TPU v7x, 128 devices: a whole 4x4x4 slice. The times are simulated.
128 devices in a mesh: wide: 16 (over z, x), narrow: 8 (over y, core).
Axes of the slice: x: 4, y: 4, z: 4, core: 2. Of those that a mesh axis runs over, the one named last changes fastest.
Arguments:
- factors: bfloat16 [768, 256, 768], P(('wide', 'narrow')), may hold values from -0.1875 to 0.1875
- integrals: bfloat16 [768, 256, 768], P(('wide', 'narrow')), may hold values from -6 to 6
- pao_energy: float32 [768, 256], replicated, may hold values from 0.3 to 4
- lmo_energy: float32 [768], replicated, may hold values from -1.5 to -0.3
- partners: int32 [768, 4], replicated, may hold values from 0 to 767, as said below
Outputs:
- auxiliary_density: float32 [768, 768], P('wide', 'narrow')
Inputs may be any that keep to these rules, and one draw needn't show every extreme that they name: LMO i is held by device i // 6, devices counted with wide outermost. Each LMO's 4 partners are LMOs other than itself, held by devices with the same narrow index as its own holder, in 4 different wide groups (its own device may be one). The listed pairs of one device's 6 LMOs point to exactly 8 devices, with exactly 3 pairs and exactly 2 distinct partners on each of them.
All inputs are finite; a program needn't handle non-finite values.
Results may differ from a plain program's by a relative error of at most 0.0035.
Values may be sent and summed in bfloat16 or wider, within the bound.
A program may use at most 128 MiB of HBM per device.

v0:
```python
import jax
import jax.numpy as jnp
from jax import lax
from jax.sharding import PartitionSpec as P

PARTNERS = 4
DISTINCT_CAP = 2


def in_blocks(value, dim, count):
    dims = value.shape
    tiles = value.reshape(*dims[:dim], count, dims[dim] // count, *dims[dim + 1 :])
    return jnp.moveaxis(tiles, dim, 0)


def sum_at_owner(value, axis, dim):
    count = lax.axis_size(axis)
    tiles = lax.all_to_all(in_blocks(value, dim, count), axis, 0, 0, tiled=True)
    return jnp.sum(tiles, axis=0)


def local(factors, integrals, pao_energy, lmo_energy, partners):
    wide_count = lax.axis_size("wide")
    narrow_count = lax.axis_size("narrow")
    wide_index = lax.axis_index("wide")
    narrow_index = lax.axis_index("narrow")
    lmo_dev, orbitals, auxiliary = factors.shape
    pair_count = lmo_dev * PARTNERS
    first_lmo = (wide_index * narrow_count + narrow_index) * lmo_dev
    listed = lax.dynamic_slice_in_dim(partners, first_lmo, lmo_dev, 0).reshape(pair_count)
    target = listed // lmo_dev // narrow_count
    target_slot = listed % lmo_dev
    column = lax.dynamic_index_in_dim(
        partners.reshape(wide_count, narrow_count, pair_count), narrow_index, 1, keepdims=False
    )
    asked_group = column // lmo_dev // narrow_count
    asked_slot = column % lmo_dev
    hits = asked_group == wide_index
    slots = DISTINCT_CAP
    local_ids = jnp.arange(lmo_dev, dtype=jnp.int32)
    wanted = jnp.any(
        hits[:, :, None] & (asked_slot[:, :, None] == local_ids[None, None, :]), axis=1
    )
    order = jnp.cumsum(wanted.astype(jnp.int32), axis=1) - 1
    picked = wanted[:, :, None] & (
        order[:, :, None] == jnp.arange(slots, dtype=jnp.int32)[None, None, :]
    )
    send_slot = jnp.sum(jnp.where(picked, local_ids[None, :, None], 0), axis=1)
    outgoing = jnp.take(factors, send_slot, axis=0)
    arrived = lax.all_to_all(outgoing, "wide", split_axis=0, concat_axis=0, tiled=True)
    needed = jnp.any(
        (target[None, :, None] == target[:, None, None])
        & (target_slot[None, :, None] == local_ids[None, None, :]),
        axis=1,
    )
    rank = jnp.sum(needed & (local_ids[None, :] < target_slot[:, None]), axis=1)
    partner = jnp.take(
        arrived.reshape(wide_count * slots, orbitals, auxiliary), target * slots + rank, axis=0
    ).reshape(lmo_dev, PARTNERS, orbitals, auxiliary)
    own_pao = lax.dynamic_slice_in_dim(pao_energy, first_lmo, lmo_dev, 0)
    other_pao = jnp.take(pao_energy, listed, axis=0).reshape(lmo_dev, PARTNERS, orbitals)
    own_lmo = lax.dynamic_slice_in_dim(lmo_energy, first_lmo, lmo_dev, 0)
    other_lmo = jnp.take(lmo_energy, listed, axis=0).reshape(lmo_dev, PARTNERS)
    denominator = (
        own_pao[:, None, :, None]
        + other_pao[:, :, None, :]
        - own_lmo[:, None, None, None]
        - other_lmo[:, :, None, None]
    )
    pair_integral = jnp.einsum(
        "sar,skbr->skab", factors, partner, preferred_element_type=jnp.float32
    )
    amplitude = (pair_integral / denominator).astype(jnp.bfloat16)
    fitted_density = jnp.einsum(
        "skab,skbr->sar", amplitude, partner, preferred_element_type=jnp.float32
    ).astype(jnp.bfloat16)
    partial_total = lax.dot_general(
        integrals.reshape(-1, auxiliary),
        fitted_density.reshape(-1, auxiliary),
        (((0,), (0,)), ((), ())),
        preferred_element_type=jnp.float32,
    )
    symmetric = 0.5 * (partial_total + partial_total.T)
    row_block = sum_at_owner(symmetric, "wide", 0)
    tile = sum_at_owner(row_block, "narrow", 1)
    return tile


def solution(mesh):
    in_specs = (P(("wide", "narrow"), None, None), P(("wide", "narrow"), None, None), P(), P(), P())
    out_specs = P("wide", "narrow")
    return jax.shard_map(local, mesh=mesh, in_specs=in_specs, out_specs=out_specs, check_vma=False)
```

profile of v0, /device:TPU:1, one launch (start us, length us, event | category | flops | bytes accessed | tf_op | source)
XLA Modules:
  0.0 299.7 jit_solution(10316477630387815695)
XLA Ops:
  0.0 0.0 copy-start
  0.0 1.0 copy.42
  1.0 0.1 reshape.411
  1.2 0.7 fusion.33
  1.9 0.2 fusion.16
  2.2 0.1 copy.47
  2.3 0.1 copy.48
  2.4 0.1 reshape.418
  2.5 0.0 copy-done
  2.5 6.5 %gather_fusion = bf16[32,256,768]{2,1,0:T(8,128)(2,1)} fusion(bf16[6,256,768]{2,1,0:T(8,128)(2,1)S(1)} %copy-done, s32[1024]{0:T(1024)S(1)} %pad_clamp_fusion.2), kind=kCustom, calls=%fused_computation | custom fusion | bytes 25165952 | tf_op jit(solution)/shard_map/jit(_take)/gather | solution.py:49
  9.1 10.9 %broadcast_select_fusion = bf16[16,2,256,768]{3,2,1,0:T(8,128)(2,1)} fusion(bf16[16,2,256,768]{3,2,1,0:T(8,128)(2,1)} %bitcast.65, pred[16,2]{1,0:T(8,128)(4,1)S(1)} %copy.47), kind=kLoop, calls=%fused_computation.4 | loop fusion | flops 6291456 | bytes 25165856 | tf_op jit(solution)/shard_map/jit(_take)/select_n | solution.py:49
  19.9 0.0 copy-start.1
  19.9 8.6 %all-to-all-start = ((bf16[16,2,256,768]{3,2,1,0:T(8,128)(2,1)}), bf16[16,2,256,768]{3,2,1,0:T(8,128)(2,1)}, u32[]{:S(2)}, u32[]{:S(2)}) async-start(bf16[16,2,256,768]{3,2,1,0:T(8,128)(2,1)} %broadcast_select_fusion), calls=%async_computation | async-start | bytes 25165824 | tf_op jit(solution)/shard_map/all_to_all | solution.py:50
  28.5 0.0 copy-done.1
  28.5 0.1 dynamic_slice.16
  28.6 0.1 ne.195
  28.7 0.1 reshape.413
  28.8 0.1 div.86
  28.9 0.1 rem.138
  29.0 0.1 broadcast_compare_fusion
  29.1 0.2 and_reduce_fusion
  29.3 0.1 reduce_sum.43
  29.4 0.7 gather_fusion.3
  30.1 0.1 gather.28
  30.2 1.7 gather_fusion.2
  31.9 0.7 constant_dynamic-slice_fusion
  32.7 0.1 broadcast_select_fusion.8
  32.8 181.0 %all-to-all-done = bf16[16,2,256,768]{3,2,1,0:T(8,128)(2,1)} async-done(((bf16[16,2,256,768]{3,2,1,0:T(8,128)(2,1)}), bf16[16,2,256,768]{3,2,1,0:T(8,128)(2,1)}, u32[]{:S(2)}, u32[]{:S(2)}) %all-to-all-start) | async-done | bytes 12582944 | tf_op jit(solution)/shard_map/all_to_all | solution.py:50
  213.8 10.3 %gather_fusion.1 = bf16[24,256,768]{2,1,0:T(8,128)(2,1)} fusion(bf16[32,256,768]{2,1,0:T(8,128)(2,1)} %bitcast.8, s32[1024]{0:T(1024)S(1)} %pad_clamp_fusion.1), kind=kCustom, calls=%fused_computation.1 | custom fusion | bytes 18874464 | tf_op jit(solution)/shard_map/jit(_take)/gather | solution.py:57
  224.1 13.4 %fusion = bf16[6,256,768,1]{2,1,3,0:T(8,128)(2,1)} fusion(bf16[6,4,256,768]{3,2,1,0:T(8,128)(2,1)} %bitcast.67, pred[6,4]{1,0:T(8,128)(4,1)S(1)} %compare_and_fusion.1, f32[6,4]{1,0:T(8,128)S(1)} %get-tuple-element.5, f32[6]{0:T(128)S(1)} %dynamic_slice.16, f32[6,4,256]{2,1,0:T(4,128)S(1)} %broadcast_select_fusion.8, ...), kind=kOutput, calls=%fused_computation.6 | convolution fusion | flops 4849139712 | bytes 14186640 | tf_op jit(solution)/shard_map/skab,skbr->sar/dot_general | solution.py:74
  237.5 5.8 %fusion.14 = f32[768,768]{1,0:T(8,128)} fusion(bf16[6,256,768]{2,1,0:T(8,128)(2,1)} %param.6, bf16[6,256,768,1]{2,1,3,0:T(8,128)(2,1)} %fusion), kind=kOutput, calls=%fused_computation.21 | convolution fusion | flops 1811939328 | bytes 7077888 | tf_op jit(solution)/shard_map/dot_general | solution.py:77
  243.3 3.1 %copy.51 = f32[768,768]{0,1:T(8,128)} copy(f32[768,768]{1,0:T(8,128)} %fusion.14) | data formatting | bytes 4718592 | tf_op jit(solution)/shard_map/dot_general | solution.py:77
  246.4 2.7 fusion.13
  249.1 34.8 %all_to_all.15 = f32[16,48,768]{2,1,0:T(8,128)} all-to-all(f32[16,48,768]{2,1,0:T(8,128)S(1)} %bitcast.66), channel_id=1, replica_groups=mesh['wide'=16,'narrow'=8] {'wide'}, dimensions={0} | all-to-all | bytes 4718592 | tf_op jit(solution)/shard_map/all_to_all | solution.py:18
  283.9 1.8 reduce_sum.47
  285.7 0.1 reshape.415
  285.8 13.2 %all_to_all.16 = f32[8,48,96]{2,1,0:T(8,128)S(1)} all-to-all(f32[8,48,96]{2,1,0:T(8,128)S(1)} %copy.52), channel_id=1, replica_groups=mesh['wide'=16,'narrow'=8] {'narrow'}, dimensions={0} | all-to-all | bytes 294912 | tf_op jit(solution)/shard_map/all_to_all | solution.py:18
  299.0 0.6 reduce_sum.48
  (22 shorter events, 0.3 us)
Async XLA Ops:
  0.0 2.5 copy-start
  19.9 8.6 %copy-start.1 = (f32[768]{0:T(1024)S(1)}, f32[768]{0:T(1024)}, u32[]{:S(2)}) copy-start(f32[768]{0:T(1024)} %param.8) | copy-start | bytes 9220
  19.9 193.9 %all-to-all-start = ((bf16[16,2,256,768]{3,2,1,0:T(8,128)(2,1)}), bf16[16,2,256,768]{3,2,1,0:T(8,128)(2,1)}, u32[]{:S(2)}, u32[]{:S(2)}) async-start(bf16[16,2,256,768]{3,2,1,0:T(8,128)(2,1)} %broadcast_select_fusion), calls=%async_computation | async-start | bytes 25165824 | tf_op jit(solution)/shard_map/all_to_all | solution.py:50
where the time goes:
time: 300 us
  waiting for transfers between devices  181 us (60%)
  blocking collectives  48 us (16%)
  local copies, waits for them, and re-layouts  25.3 us (8%)
  matrix products  19.2 us (6%)
  other arithmetic  17.4 us (6%)
  starting transfers between devices  8.6 us (3%)
    all_to_all x1, waiting for transfers between devices, local(): lax.all_to_all(outgoing, 'wide', split_axis=0, concat_axis=0, tiled=True)  181 us
    all_to_all x2, blocking collectives, sum_at_owner(): tiles = lax.all_to_all(in_blocks(value, dim, count), axis, 0, 0, tiled=True)  48 us
    dot_general x1, matrix products, local(): jnp.einsum('skab,skbr->sar', amplitude, partner, preferred_element_type=j...  13.4 us
    select_n x2, other arithmetic, local(): outgoing = jnp.take(factors, send_slot, axis=0)  10.9 us
    gather x1, local copies, waits for them, and re-layouts, local(): jnp.take(arrived.reshape(wide_count * slots, orbitals, auxiliary), target...  10.3 us
    all_to_all x1, starting transfers between devices, local(): lax.all_to_all(outgoing, 'wide', split_axis=0, concat_axis=0, tiled=True)  8.6 us
    gather x1, local copies, waits for them, and re-layouts, local(): outgoing = jnp.take(factors, send_slot, axis=0)  6.54 us
  transfers between devices with their start and end apart: 1, of which 1 were waited for; matrix products, arithmetic and copies ran while one was open for 1% of the time, Pallas kernels for 0%

commit v1 on v0

v1 whole, which is shorter than its diff:
```python
import functools

import jax
import jax.numpy as jnp
import numpy as np
from jax import lax
from jax.experimental import pallas as pl
from jax.experimental.pallas import tpu as pltpu
from jax.sharding import PartitionSpec as P

MESH = pl.DeviceIdType.MESH
LMO = 6
PARTNERS = 4
PAIRS = LMO * PARTNERS
PAO = 256
AUX = 768
ROTS = 4
PIECE = PAO // ROTS

MASKS = (1, 4, 3, 12)


def order(rot):
    return [MASKS[(rot + step) % 4] for step in range(4)]


def flip(position, mask):
    if mask == 0:
        return position
    if mask == 3:
        return 3 - position
    return position + 1 - 2 * lax.rem(position, 2)


def neighbour(mask):
    wide = lax.axis_index("wide")
    z, x = wide // 4, lax.rem(wide, 4)
    return (flip(z, mask // 4) * 4 + flip(x, mask % 4), lax.axis_index("narrow"))


def kernel(table, factors, integrals, own_energy, other_energy, total, *scratch):
    row = list(scratch[0:4])
    send3 = list(scratch[4:8])
    send4 = list(scratch[8:12])
    passing = list(scratch[12:16])
    final = list(scratch[16:20])
    flipped, fitted, energy, local_sem, send_sem, recv_sem = scratch[20:]

    barrier = pltpu.get_barrier_semaphore()
    for mask in MASKS:
        pl.semaphore_signal(barrier, inc=1, device_id=neighbour(mask), device_id_type=MESH)
    pl.semaphore_wait(barrier, 4)

    def copy(rot, kind, src, dst, mask):
        return pltpu.make_async_remote_copy(
            src_ref=src,
            dst_ref=dst,
            send_sem=send_sem.at[rot, kind],
            recv_sem=recv_sem.at[rot, kind],
            device_id=neighbour(mask),
            device_id_type=MESH,
        )

    copies = []
    for rot in range(ROTS):
        m1, m2, m3, m4 = order(rot)
        own = factors.at[:, pl.ds(rot * PIECE, PIECE), :]
        copies.append(
            [
                copy(rot, 0, own, row[rot].at[pl.ds(6, 6)], m1),
                copy(rot, 1, own, row[rot].at[pl.ds(12, 6)], m2),
                copy(rot, 2, row[rot].at[pl.ds(6, 6)], row[rot].at[pl.ds(18, 6)], m2),
                copy(rot, 3, send3[rot].at[1], passing[rot], m3),
                copy(rot, 4, send3[rot].at[0], final[rot].at[pl.ds(8, 8)], m3),
                copy(rot, 5, send4[rot], final[rot].at[pl.ds(16, 8)], m4),
                copy(rot, 6, passing[rot], final[rot].at[pl.ds(24, 8)], m4),
            ]
        )
    for rot in range(ROTS):
        copies[rot][0].start()
    for rot in range(ROTS):
        copies[rot][1].start()
    local = []
    for rot in range(ROTS):
        own = factors.at[:, pl.ds(rot * PIECE, PIECE), :]
        local.append(pltpu.make_async_copy(own, row[rot].at[pl.ds(0, 6)], local_sem.at[rot]))
        local[rot].start()

    columns = jnp.transpose(own_energy[...])
    for i in range(LMO):
        energy[i] = jnp.broadcast_to(columns[:, i : i + 1], (PAO, PAO))
        flipped[:, i * PAO : (i + 1) * PAO] = jnp.transpose(integrals[i])

    for rot in range(ROTS):
        copies[rot][0].wait_recv()
        copies[rot][2].start()

    def gather(rot, receiver, put):
        def body(slot, carry):
            put(slot, row[rot][table[rot * 32 + receiver * 8 + slot]])
            return carry

        lax.fori_loop(0, 8, body, 0)

    def put_into(ref, base):
        def put(slot, value):
            ref[base + slot] = value

        return put

    def put_send3(rot, which):
        def put(slot, value):
            send3[rot][which, slot] = value

        return put

    for rot in range(ROTS):
        local[rot].wait()
        copies[rot][1].wait_recv()
        copies[rot][2].wait_recv()
        gather(rot, 1, put_send3(rot, 1))
        copies[rot][3].start()
    for rot in range(ROTS):
        gather(rot, 0, put_send3(rot, 0))
        copies[rot][4].start()
        gather(rot, 2, put_into(send4[rot], 0))
        copies[rot][5].start()
    for rot in range(ROTS):
        gather(rot, 3, put_into(final[rot], 0))
    for rot in range(ROTS):
        copies[rot][3].wait_recv()
        copies[rot][6].start()
    for rot in range(ROTS):
        for kind in (4, 5, 6):
            copies[rot][kind].wait_recv()

    def one(i, carry):
        mine = factors[i]
        gathered = jnp.zeros((PAO, AUX), jnp.float32)
        for k in range(PARTNERS):
            pair = i * PARTNERS + k
            other = jnp.concatenate(
                [final[rot][table[128 + rot * PAIRS + pair]] for rot in range(ROTS)], axis=0
            )
            integral = lax.dot_general(
                mine, other, (((1,), (1,)), ((), ())), preferred_element_type=jnp.float32
            )
            amplitude = (integral / (energy[i] + other_energy[pair])).astype(jnp.bfloat16)
            gathered = gathered + jnp.dot(amplitude, other, preferred_element_type=jnp.float32)
        fitted[pl.ds(pl.multiple_of(i * PAO, PAO), PAO), :] = gathered.astype(jnp.bfloat16)
        return carry

    lax.fori_loop(0, LMO, one, 0)

    def rows(block, carry):
        at = pl.ds(pl.multiple_of(block * 256, 256), 256)
        total[at, :] = jnp.dot(flipped[at, :], fitted[...], preferred_element_type=jnp.float32)
        return carry

    lax.fori_loop(0, AUX // 256, rows, 0)

    for rot in range(ROTS):
        for kind in range(7):
            copies[rot][kind].wait_send()


def exchange_and_multiply(table, factors, integrals, own_energy, other_energy):
    vmem = pl.BlockSpec(memory_space=pltpu.VMEM)
    piece = (PIECE, AUX)
    scratch = []
    for shape in ((24,), (2, 8), (8,), (8,), (32,)):
        scratch += [pltpu.VMEM(shape + piece, jnp.bfloat16) for _ in range(ROTS)]
    scratch += [
        pltpu.VMEM((AUX, LMO * PAO), jnp.bfloat16),
        pltpu.VMEM((LMO * PAO, AUX), jnp.bfloat16),
        pltpu.VMEM((LMO, PAO, PAO), jnp.float32),
        pltpu.SemaphoreType.DMA((ROTS,)),
        pltpu.SemaphoreType.DMA((ROTS, 7)),
        pltpu.SemaphoreType.DMA((ROTS, 7)),
    ]
    return pl.pallas_call(
        kernel,
        out_shape=jax.ShapeDtypeStruct((AUX, AUX), jnp.float32),
        in_specs=[pl.BlockSpec(memory_space=pltpu.SMEM), vmem, vmem, vmem, vmem],
        out_specs=vmem,
        scratch_shapes=scratch,
        compiler_params=pltpu.CompilerParams(
            collective_id=0, has_side_effects=True, vmem_limit_bytes=60 * 2**20
        ),
    )(table, factors, integrals, own_energy, other_energy)


def make_table(column, wide_index):
    relative = jnp.take(column, wide_index ^ jnp.arange(16, dtype=jnp.int32), axis=0)
    source = (relative // (LMO * 8)) ^ wide_index
    slot = relative % LMO
    at = source[:, None, :] == jnp.arange(16, dtype=jnp.int32)[None, :, None]
    low = jnp.min(jnp.where(at, slot[:, None, :], LMO - 1), axis=2)
    high = jnp.max(jnp.where(at, slot[:, None, :], 0), axis=2)
    wanted = jnp.stack([low, high], axis=-1).reshape(-1)
    pick, base = [], []
    for rot in range(ROTS):
        m1, m2, m3, m4 = order(rot)
        for receiver in (m3, m3 ^ m4, m4, 0):
            for q in range(4):
                sender = (m1 if q & 1 else 0) ^ (m2 if q & 2 else 0)
                for k in range(2):
                    pick.append((receiver * 16 + sender) * 2 + k)
                    base.append(q * LMO)
    sends = wanted[np.array(pick)] + np.array(base, np.int32)

    mine, mine_slot = source[0], slot[0]
    is_high = mine_slot == jnp.sum(jnp.where(at[0], high[0][:, None], 0), axis=0)
    digit = {}
    for low_mask, high_mask, part in ((1, 3, mine % 4), (4, 12, mine // 4)):
        digit[low_mask] = ((part == 1) | (part == 2)).astype(jnp.int32)
        digit[high_mask] = ((part == 3) | (part == 2)).astype(jnp.int32)
    places = []
    for rot in range(ROTS):
        m1, m2, m3, m4 = order(rot)
        group = digit[m3] + 2 * digit[m4]
        places.append((group * 4 + digit[m1] + 2 * digit[m2]) * 2 + is_high.astype(jnp.int32))
    return jnp.concatenate([sends] + places).astype(jnp.int32)


def in_blocks(value, dim, count):
    dims = value.shape
    tiles = value.reshape(*dims[:dim], count, dims[dim] // count, *dims[dim + 1 :])
    return jnp.moveaxis(tiles, dim, 0)


def sum_at_owner(value, axis, dim):
    count = lax.axis_size(axis)
    tiles = lax.all_to_all(in_blocks(value, dim, count), axis, 0, 0, tiled=True)
    return jnp.sum(tiles, axis=0)


def local(factors, integrals, pao_energy, lmo_energy, partners):
    wide_index = lax.axis_index("wide")
    narrow_index = lax.axis_index("narrow")
    first_lmo = (wide_index * 8 + narrow_index) * LMO
    column = lax.dynamic_index_in_dim(
        partners.reshape(16, 8, PAIRS), narrow_index, 1, keepdims=False
    )
    table = make_table(column, wide_index)
    listed = lax.dynamic_slice_in_dim(partners, first_lmo, LMO, 0).reshape(PAIRS)
    shifted = pao_energy - lmo_energy[:, None]
    own_energy = lax.dynamic_slice_in_dim(shifted, first_lmo, LMO, 0)
    own_energy = jnp.pad(own_energy, ((0, 8 - LMO), (0, 0)))
    other_energy = jnp.take(shifted, listed, axis=0).reshape(PAIRS, 1, PAO)
    partial_total = exchange_and_multiply(table, factors, integrals, own_energy, other_energy)
    symmetric = 0.5 * (partial_total + partial_total.T)
    row_block = sum_at_owner(symmetric, "wide", 0)
    return sum_at_owner(row_block, "narrow", 1)


def solution(mesh):
    in_specs = (P(("wide", "narrow"), None, None), P(("wide", "narrow"), None, None), P(), P(), P())
    out_specs = P("wide", "narrow")
    return jax.shard_map(local, mesh=mesh, in_specs=in_specs, out_specs=out_specs, check_vma=False)
```

time: 300 us -> 193 us (0.64)
  waiting for transfers between devices: 181 us -> 0 us
  Pallas kernels: 0 us -> 129 us
  matrix products: 19.2 us -> 0 us
  local copies, waits for them, and re-layouts: 25.3 us -> 9.44 us
  other arithmetic: 17.4 us -> 6.27 us
  starting transfers between devices: 8.6 us -> 0 us
    all_to_all x1 -> x0, waiting for transfers between devices: 181 us -> none  [local(): lax.all_to_all(outgoing, 'wide', split_axis=0, concat_axis=0, tiled=True)]
    pallas_call x0 -> x1, Pallas kernels: none -> 129 us  [exchange_and_multiply(): pl.pallas_call(kernel, out_shape=jax.ShapeDtypeStruct((AUX, AUX), jnp.flo...]
    dot_general x2 -> x0, matrix products: 19.2 us -> none  [the longest x1 13.4 us: local(): jnp.einsum('skab,skbr->sar', amplitude, partner, preferred_element_type=j...]
    gather x6 -> x3, local copies, waits for them, and re-layouts: 19.4 us -> 2.42 us  [the longest x1 1.27 us: make_table(): sends = wanted[np.array(pick)] + np.array(base, np.int32)]
    select_n x7 -> x3, other arithmetic: 11 us -> 0.71 us  [the longest x2 0.71 us: local(): other_energy = jnp.take(shifted, listed, axis=0).reshape(PAIRS, 1, PAO)]
    all_to_all x1 -> x0, starting transfers between devices: 8.6 us -> none  [local(): lax.all_to_all(outgoing, 'wide', split_axis=0, concat_axis=0, tiled=True)]
    pallas_call x0 -> x1, local copies, waits for them, and re-layouts: none -> 3.19 us  [exchange_and_multiply(): pl.pallas_call(kernel, out_shape=jax.ShapeDtypeStruct((AUX, AUX), jnp.flo...]
    dot_general x1 -> x0, local copies, waits for them, and re-layouts: 3.07 us -> none  [local(): lax.dot_general(integrals.reshape(-1, auxiliary), fitted_density.reshape(...]
  transfers between devices with their start and end apart: 1 -> 0, of which waited for: 1 -> 0; matrix products, arithmetic and copies ran while one was open for 1% -> 0% of each run, Pallas kernels for 0% -> 0%
where the time goes in v1:
time: 193 us; the launch traced here: 192 us
  Pallas kernels  129 us (67%)
  blocking collectives  47.5 us (25%)
  local copies, waits for them, and re-layouts  9.44 us (5%)
  other arithmetic  6.27 us (3%)
    pallas_call x1, Pallas kernels, exchange_and_multiply(): pl.pallas_call(kernel, out_shape=jax.ShapeDtypeStruct((AUX, AUX), jnp.flo...  129 us
    all_to_all x2, blocking collectives, sum_at_owner(): tiles = lax.all_to_all(in_blocks(value, dim, count), axis, 0, 0, tiled=True)  47.5 us

profile of v1, /device:TPU:1, one launch (start us, length us, event | category | flops | bytes accessed | tf_op | source)
XLA Modules:
  0.0 192.2 jit_solution(6543527687998170145)
XLA Ops:
  0.0 0.0 copy-start.1
  0.0 0.8 constant_dynamic-slice_fusion
  0.8 0.1 copy.24
  0.9 0.1 reshape.139
  1.0 0.1 reshape.138
  1.1 0.9 copy.22
  2.0 0.7 pad_clamp_fusion.1
  2.7 0.1 reshape.136
  2.8 0.6 gather_fusion
  3.4 0.1 fusion.1
  3.5 0.6 select_reduce_fusion.1
  4.2 0.1 select_reduce_fusion.2
  4.3 0.2 copy.23
  4.5 0.1 reshape.137
  4.6 1.3 broadcast_subtract_fusion
  5.9 0.6 gather_fusion.2
  6.5 1.3 gather_fusion.1
  7.8 0.0 copy-done.1
  7.8 0.7 broadcast_select_fusion.other_energy
  8.5 0.6 pad.4.own_energy
  9.1 0.7 concatenate.3.table
  9.8 128.8 %shard_map.82 = f32[768,768]{1,0:T(8,128)} custom-call(s32[224]{0:T(256)} %concatenate.3.table, bf16[6,256,768]{2,1,0:T(8,128)(2,1)} %factors.1, bf16[6,256,768]{2,1,0:T(8,128)(2,1)} %integrals.1, f32[8,256]{1,0:T(8,128)} %pad.4.own_energy, f32[24,1,256]{2,1,0:T(1,128)} %broadcast_select_fusion.other_energy), custom_call_target="tpu_custom_call" | custom-call | tf_op jit(solution)/shard_map/pallas_call | solution.py:181
  138.6 0.0 copy-start
  138.6 3.2 %copy.26 = f32[768,768]{0,1:T(8,128)} copy(f32[768,768]{1,0:T(8,128)} %shard_map.82) | data formatting | bytes 4718592 | tf_op jit(solution)/shard_map/pallas_call | solution.py:181
  141.8 0.0 copy-done
  141.8 2.0 %fusion = f32[768,768]{1,0:T(8,128)S(1)} fusion(f32[768,768]{1,0:T(8,128)S(1)} %copy-done, f32[768,768]{0,1:T(8,128)} %copy.26), kind=kLoop, calls=%fused_computation.4 | loop fusion | flops 1179648 | bytes 7077888 | tf_op jit(solution)/shard_map/mul | solution.py:252
  143.8 33.7 %all_to_all.10 = f32[16,48,768]{2,1,0:T(8,128)S(1)} all-to-all(f32[16,48,768]{2,1,0:T(8,128)S(1)} %bitcast.32), channel_id=1, replica_groups=mesh['wide'=16,'narrow'=8] {'wide'}, dimensions={0} | all-to-all | bytes 4718592 | tf_op jit(solution)/shard_map/all_to_all | solution.py:234
  177.5 0.1 reduce_sum.28
  177.6 0.1 reshape.141
  177.8 13.8 %all_to_all.11 = f32[8,48,96]{2,1,0:T(8,128)S(1)} all-to-all(f32[8,48,96]{2,1,0:T(8,128)S(1)} %copy.27), channel_id=1, replica_groups=mesh['wide'=16,'narrow'=8] {'narrow'}, dimensions={0} | all-to-all | bytes 294912 | tf_op jit(solution)/shard_map/all_to_all | solution.py:234
  191.6 0.6 reduce_sum.29
  (15 shorter events, 0.2 us)
Async XLA Ops:
  0.0 7.8 %copy-start.1 = (s32[128]{0:T(128)S(1)}, s32[128]{0:T(128)}, u32[]{:S(2)}) copy-start(s32[128]{0:T(128)} %constant.122.clone) | copy-start | bytes 1540
  138.6 3.2 %copy-start = (f32[768,768]{1,0:T(8,128)S(1)}, f32[768,768]{1,0:T(8,128)}, u32[]{:S(2)}) copy-start(f32[768,768]{1,0:T(8,128)} %shard_map.82) | copy-start | bytes 7077892

commit v2 on v1

--- a/solution.py
+++ b/solution.py
@@ -14,6 +14,8 @@
 PAIRS = LMO * PARTNERS
 PAO = 256
 AUX = 768
+ROWS = AUX // 8
+HEIGHT = AUX // 16
 ROTS = 4
 PIECE = PAO // ROTS
 
@@ -29,6 +31,8 @@
         return position
     if mask == 3:
         return 3 - position
+    if mask == 2:
+        return lax.rem(position + 2, 4)
     return position + 1 - 2 * lax.rem(position, 2)
 
 
@@ -38,18 +42,112 @@
     return (flip(z, mask // 4) * 4 + flip(x, mask % 4), lax.axis_index("narrow"))
 
 
-def kernel(table, factors, integrals, own_energy, other_energy, total, *scratch):
+def along_y(mask, core=0):
+    narrow = lax.axis_index("narrow")
+    y, c = narrow // 2, lax.rem(narrow, 2)
+    return (lax.axis_index("wide"), flip(y, mask) * 2 + flip(c, core))
+
+
+def reduce_total(
+    tile, total, core_in, summed, first_out, first_in, second_out, second_in, block, turned, tiles_in,
+    core_sem, y_sem, wide_sem,
+):
+    narrow, wide = lax.axis_index("narrow"), lax.axis_index("wide")
+    y, core = narrow // 2, lax.rem(narrow, 2)
+
+    def send(src, dst, sems, device):
+        return pltpu.make_async_remote_copy(
+            src_ref=src, dst_ref=dst, send_sem=sems[0], recv_sem=sems[1],
+            device_id=device, device_id_type=MESH,
+        )
+
+    for i in range(3):
+        for j in range(i, 3):
+            at_i, at_j = slice(i * 256, i * 256 + 256), slice(j * 256, j * 256 + 256)
+            half = 0.5 * (total[at_i, at_j] + jnp.transpose(total[at_j, at_i]))
+            total[at_i, at_j] = half
+            if i != j:
+                total[at_j, at_i] = jnp.transpose(half)
+
+    def band(u, c):
+        return pl.ds(pl.multiple_of((flip(y, u) * 2 + c) * ROWS, ROWS), ROWS)
+
+    steps = []
+    for u in range(4):
+        steps.append(
+            send(total.at[band(u, 1 - core)], core_in.at[u],
+                 (core_sem.at[0, u], core_sem.at[1, u]), along_y(0, 1))
+        )
+        steps[u].start()
+    for u in (1, 2, 3, 0):
+        steps[u].wait_recv()
+        summed[u] = total[band(u, core), :] + core_in[u]
+
+    left, right = slice(0, AUX // 2), slice(AUX // 2, AUX)
+    plan = ((left, 1, 3, (1, 2)), (right, 3, 1, (3, 2)))
+    firsts, seconds = [], []
+    for h, (columns, near, far, sent) in enumerate(plan):
+        for slot, u in enumerate(sent):
+            first_out[h, slot] = summed[u, :, columns].astype(first_out.dtype)
+        firsts.append(
+            send(first_out.at[h], first_in.at[h], (y_sem.at[0, h], y_sem.at[1, h]), along_y(near))
+        )
+        firsts[h].start()
+    for h, (columns, near, far, sent) in enumerate(plan):
+        firsts[h].wait_recv()
+        passed = summed[far, :, columns] + first_in[h, 1].astype(jnp.float32)
+        second_out[h] = passed.astype(second_out.dtype)
+        seconds.append(
+            send(second_out.at[h], second_in.at[h], (y_sem.at[2, h], y_sem.at[3, h]), along_y(far))
+        )
+        seconds[h].start()
+    block[pl.ds(ROWS, 128 - ROWS), :] = jnp.zeros((128 - ROWS, AUX), jnp.float32)
+    for h, (columns, near, far, sent) in enumerate(plan):
+        kept = summed[0, :, columns] + first_in[h, 0].astype(jnp.float32)
+        seconds[h].wait_recv()
+        block[pl.ds(0, ROWS), columns] = kept + second_in[h].astype(jnp.float32)
+
+    for j in range(AUX // 128):
+        at = slice(j * 128, j * 128 + 128)
+        turned[at, :] = jnp.transpose(block[:, at])
+
+    def rows(t):
+        peer = flip(wide // 4, t // 4) * 4 + flip(lax.rem(wide, 4), t % 4)
+        return pl.ds(pl.multiple_of(peer * HEIGHT, HEIGHT), HEIGHT)
+
+    spread = []
+    for t in range(1, 16):
+        spread.append(
+            send(turned.at[rows(t)], tiles_in.at[t - 1],
+                 (wide_sem.at[0, t - 1], wide_sem.at[1, t - 1]), neighbour(t))
+        )
+        spread[-1].start()
+    result = turned[rows(0), :]
+    for t in range(1, 16):
+        spread[t - 1].wait_recv()
+        result = result + tiles_in[t - 1]
+    tile[...] = result[:, :ROWS]
+
+    for step in steps + firsts + seconds + spread:
+        step.wait_send()
+
+
+def kernel(table, factors, integrals, own_energy, other_energy, tile, *scratch):
     row = list(scratch[0:4])
     send3 = list(scratch[4:8])
     send4 = list(scratch[8:12])
     passing = list(scratch[12:16])
     final = list(scratch[16:20])
-    flipped, fitted, energy, local_sem, send_sem, recv_sem = scratch[20:]
+    flipped, fitted, energy, local_sem, send_sem, recv_sem = scratch[20:26]
+    reduction = scratch[26:]
+    total = reduction[0]
 
     barrier = pltpu.get_barrier_semaphore()
-    for mask in MASKS:
-        pl.semaphore_signal(barrier, inc=1, device_id=neighbour(mask), device_id_type=MESH)
-    pl.semaphore_wait(barrier, 4)
+    greeted = [neighbour(mask) for mask in range(1, 16)]
+    greeted += [along_y(0, 1), along_y(1), along_y(3)]
+    for device in greeted:
+        pl.semaphore_signal(barrier, inc=1, device_id=device, device_id_type=MESH)
+    pl.semaphore_wait(barrier, len(greeted))
 
     def copy(rot, kind, src, dst, mask):
         return pltpu.make_async_remote_copy(
@@ -159,6 +257,8 @@
 
     lax.fori_loop(0, AUX // 256, rows, 0)
 
+    reduce_total(tile, *reduction)
+
     for rot in range(ROTS):
         for kind in range(7):
             copies[rot][kind].wait_send()
@@ -177,10 +277,23 @@
         pltpu.SemaphoreType.DMA((ROTS,)),
         pltpu.SemaphoreType.DMA((ROTS, 7)),
         pltpu.SemaphoreType.DMA((ROTS, 7)),
+        pltpu.VMEM((AUX, AUX), jnp.float32),
+        pltpu.VMEM((4, ROWS, AUX), jnp.float32),
+        pltpu.VMEM((4, ROWS, AUX), jnp.float32),
+        pltpu.VMEM((2, 2, ROWS, AUX // 2), jnp.bfloat16),
+        pltpu.VMEM((2, 2, ROWS, AUX // 2), jnp.bfloat16),
+        pltpu.VMEM((2, ROWS, AUX // 2), jnp.bfloat16),
+        pltpu.VMEM((2, ROWS, AUX // 2), jnp.bfloat16),
+        pltpu.VMEM((128, AUX), jnp.float32),
+        pltpu.VMEM((AUX, 128), jnp.float32),
+        pltpu.VMEM((15, HEIGHT, 128), jnp.float32),
+        pltpu.SemaphoreType.DMA((2, 4)),
+        pltpu.SemaphoreType.DMA((4, 2)),
+        pltpu.SemaphoreType.DMA((2, 15)),
     ]
     return pl.pallas_call(
         kernel,
-        out_shape=jax.ShapeDtypeStruct((AUX, AUX), jnp.float32),
+        out_shape=jax.ShapeDtypeStruct((HEIGHT, ROWS), jnp.float32),
         in_specs=[pl.BlockSpec(memory_space=pltpu.SMEM), vmem, vmem, vmem, vmem],
         out_specs=vmem,
         scratch_shapes=scratch,
@@ -221,18 +334,6 @@
         group = digit[m3] + 2 * digit[m4]
         places.append((group * 4 + digit[m1] + 2 * digit[m2]) * 2 + is_high.astype(jnp.int32))
     return jnp.concatenate([sends] + places).astype(jnp.int32)
-
-
-def in_blocks(value, dim, count):
-    dims = value.shape
-    tiles = value.reshape(*dims[:dim], count, dims[dim] // count, *dims[dim + 1 :])
-    return jnp.moveaxis(tiles, dim, 0)
-
-
-def sum_at_owner(value, axis, dim):
-    count = lax.axis_size(axis)
-    tiles = lax.all_to_all(in_blocks(value, dim, count), axis, 0, 0, tiled=True)
-    return jnp.sum(tiles, axis=0)
 
 
 def local(factors, integrals, pao_energy, lmo_energy, partners):
@@ -248,10 +349,7 @@
     own_energy = lax.dynamic_slice_in_dim(shifted, first_lmo, LMO, 0)
     own_energy = jnp.pad(own_energy, ((0, 8 - LMO), (0, 0)))
     other_energy = jnp.take(shifted, listed, axis=0).reshape(PAIRS, 1, PAO)
-    partial_total = exchange_and_multiply(table, factors, integrals, own_energy, other_energy)
-    symmetric = 0.5 * (partial_total + partial_total.T)
-    row_block = sum_at_owner(symmetric, "wide", 0)
-    return sum_at_owner(row_block, "narrow", 1)
+    return exchange_and_multiply(table, factors, integrals, own_energy, other_energy)
 
 
 def solution(mesh):

time: 193 us -> 163 us (0.84)
  blocking collectives: 47.5 us -> 0 us
  Pallas kernels: 129 us -> 152 us
  other arithmetic: 6.27 us -> 3.77 us
  local copies, waits for them, and re-layouts: 9.44 us -> 7.48 us
    all_to_all x2 -> x0, blocking collectives: 47.5 us -> none  [sum_at_owner(): tiles = lax.all_to_all(in_blocks(value, dim, count), axis, 0, 0, tiled=True)]
    pallas_call x1, Pallas kernels: 129 us -> 152 us  [exchange_and_multiply(): pl.pallas_call(kernel, out_shape=jax.ShapeDtypeStruct((HEIGHT, ROWS), jnp...]
    pallas_call x1 -> x0, local copies, waits for them, and re-layouts: 3.19 us -> none  [exchange_and_multiply(): pl.pallas_call(kernel, out_shape=jax.ShapeDtypeStruct((AUX, AUX), jnp.flo...]
    mul x1 -> x0, other arithmetic: 1.95 us -> none  [local(): symmetric = 0.5 * (partial_total + partial_total.T)]
where the time goes in v2:
time: 163 us
  Pallas kernels  152 us (93%)
  local copies, waits for them, and re-layouts  7.48 us (5%)
  other arithmetic  3.77 us (2%)
    pallas_call x1, Pallas kernels, exchange_and_multiply(): pl.pallas_call(kernel, out_shape=jax.ShapeDtypeStruct((HEIGHT, ROWS), jnp...  152 us

profile of v2, /device:TPU:1, one launch (start us, length us, event | category | flops | bytes accessed | tf_op | source)
XLA Modules:
  0.0 162.9 jit_solution(108907220491412186)
XLA Ops:
  0.0 0.0 copy-start
  0.0 0.8 constant_dynamic-slice_fusion
  0.9 0.1 copy.13
  1.0 0.1 reshape.133
  1.0 0.1 reshape.132
  1.2 0.7 pad_clamp_fusion.1
  1.8 0.9 copy.11
  2.7 0.1 reshape.130
  2.9 0.6 gather_fusion
  3.5 0.1 fusion
  3.6 0.6 select_reduce_fusion.1
  4.2 0.1 select_reduce_fusion.2
  4.4 0.2 copy.12
  4.5 0.1 reshape.131
  4.7 1.3 gather_fusion.1
  5.9 0.7 add.128
  6.6 0.7 concatenate.3.table
  7.3 0.0 copy-done
  7.3 0.9 broadcast_subtract_fusion
  8.1 0.6 gather_fusion.2
  8.7 0.7 broadcast_select_fusion.other_energy
  9.4 0.6 pad.4.own_energy
  10.0 151.5 %shard_map.82 = f32[48,96]{1,0:T(8,128)} custom-call(s32[224]{0:T(256)} %concatenate.3.table, bf16[6,256,768]{2,1,0:T(8,128)(2,1)} %factors.1, bf16[6,256,768]{2,1,0:T(8,128)(2,1)} %integrals.1, f32[8,256]{1,0:T(8,128)} %pad.4.own_energy, f32[24,1,256]{2,1,0:T(1,128)} %broadcast_select_fusion.other_energy), custom_call_target="tpu_custom_call" | custom-call | tf_op jit(solution)/shard_map/pallas_call | solution.py:294
  161.6 1.3 copy.16
  (13 shorter events, 0.1 us)
Async XLA Ops:
  0.0 7.3 %copy-start = (f32[768,256]{1,0:T(8,128)S(1)}, f32[768,256]{1,0:T(8,128)}, u32[]{:S(2)}) copy-start(f32[768,256]{1,0:T(8,128)} %param.10) | copy-start | bytes 2359300

commit v3 on v2

--- a/solution.py
+++ b/solution.py
@@ -1,8 +1,5 @@
-import functools
-
 import jax
 import jax.numpy as jnp
-import numpy as np
 from jax import lax
 from jax.experimental import pallas as pl
 from jax.experimental.pallas import tpu as pltpu
@@ -132,14 +129,87 @@
         step.wait_send()
 
 
-def kernel(table, factors, integrals, own_energy, other_energy, tile, *scratch):
+def fill_table(table, source, slot, partners):
+    wide, narrow = lax.axis_index("wide"), lax.axis_index("narrow")
+    z, x = wide // 4, lax.rem(wide, 4)
+
+    def group(mask):
+        return flip(z, mask // 4) * 4 + flip(x, mask % 4)
+
+    for rot in range(ROTS):
+        m1, m2, m3, m4 = order(rot)
+        senders = [group(mask) for mask in (0, m1, m2, m1 ^ m2)]
+        for receiver, mask in enumerate((m3, m3 ^ m4, m4, 0)):
+            first = (group(mask) * 8 + narrow) * LMO
+
+            def scan(i, found):
+                found = list(found)
+                for k in range(PARTNERS):
+                    listed = partners[k, first + i]
+                    owner = lax.div(listed, LMO)
+                    place = listed - owner * LMO
+                    holder = lax.div(owner, 8)
+                    for q in range(4):
+                        hit = holder == senders[q]
+                        low, high = found[2 * q], found[2 * q + 1]
+                        found[2 * q] = jnp.where(hit, jnp.minimum(low, place), low)
+                        found[2 * q + 1] = jnp.where(hit, jnp.maximum(high, place), high)
+                return tuple(found)
+
+            found = lax.fori_loop(0, LMO, scan, (jnp.int32(LMO - 1), jnp.int32(0)) * 4)
+            for q in range(4):
+                for k in range(2):
+                    base = q * LMO if q < 3 else 0
+                    table[rot * 32 + receiver * 8 + q * 2 + k] = found[2 * q + k] + base
+
+    first = (wide * 8 + narrow) * LMO
+
+    def split(i, carry):
+        for k in range(PARTNERS):
+            listed = partners[k, first + i]
+            owner = lax.div(listed, LMO)
+            source[i * PARTNERS + k] = lax.div(owner, 8)
+            slot[i * PARTNERS + k] = listed - owner * LMO
+        return carry
+
+    lax.fori_loop(0, LMO, split, 0)
+
+    def place(pair, carry):
+        mine, mine_slot = source[pair], slot[pair]
+
+        def larger(i, most):
+            for k in range(PARTNERS):
+                there = slot[i * PARTNERS + k]
+                most = jnp.where(source[i * PARTNERS + k] == mine, jnp.maximum(most, there), most)
+            return most
+
+        most = lax.fori_loop(0, LMO, larger, jnp.int32(0))
+        is_high = jnp.where(mine_slot == most, 1, 0)
+        sz = lax.div(mine, 4)
+        sx = mine - sz * 4
+        digit = {}
+        for low_mask, high_mask, here, there in ((1, 3, x, sx), (4, 12, z, sz)):
+            digit[low_mask] = jnp.where((flip(here, 1) == there) | (flip(here, 2) == there), 1, 0)
+            digit[high_mask] = jnp.where((flip(here, 3) == there) | (flip(here, 2) == there), 1, 0)
+        for rot in range(ROTS):
+            m1, m2, m3, m4 = order(rot)
+            block = (digit[m3] + 2 * digit[m4]) * 4 + digit[m1] + 2 * digit[m2]
+            table[128 + rot * PAIRS + pair] = block * 2 + is_high
+        return carry
+
+    lax.fori_loop(0, PAIRS, place, 0)
+
+
+def kernel(partners, lmo_energy, factors, integrals, pao_energy, tile, *scratch):
     row = list(scratch[0:4])
-    send3 = list(scratch[4:8])
-    send4 = list(scratch[8:12])
-    passing = list(scratch[12:16])
-    final = list(scratch[16:20])
-    flipped, fitted, energy, local_sem, send_sem, recv_sem = scratch[20:26]
-    reduction = scratch[26:]
+    last = list(scratch[4:8])
+    send3 = list(scratch[8:12])
+    send4 = list(scratch[12:16])
+    passing = list(scratch[16:20])
+    final = list(scratch[20:24])
+    (table, source, slot, resident, own_rows, other_energy, flipped, fitted, energy,
+     local_sem, send_sem, recv_sem) = scratch[24:36]
+    reduction = scratch[36:]
     total = reduction[0]
 
     barrier = pltpu.get_barrier_semaphore()
@@ -159,6 +229,7 @@
             device_id_type=MESH,
         )
 
+    early, late = pl.ds(0, 6), pl.ds(6, 2)
     copies = []
     for rot in range(ROTS):
         m1, m2, m3, m4 = order(rot)
@@ -167,11 +238,15 @@
             [
                 copy(rot, 0, own, row[rot].at[pl.ds(6, 6)], m1),
                 copy(rot, 1, own, row[rot].at[pl.ds(12, 6)], m2),
-                copy(rot, 2, row[rot].at[pl.ds(6, 6)], row[rot].at[pl.ds(18, 6)], m2),
-                copy(rot, 3, send3[rot].at[1], passing[rot], m3),
-                copy(rot, 4, send3[rot].at[0], final[rot].at[pl.ds(8, 8)], m3),
-                copy(rot, 5, send4[rot], final[rot].at[pl.ds(16, 8)], m4),
-                copy(rot, 6, passing[rot], final[rot].at[pl.ds(24, 8)], m4),
+                copy(rot, 2, row[rot].at[pl.ds(6, 6)], last[rot], m2),
+                copy(rot, 3, send3[rot].at[1, early], passing[rot].at[early], m3),
+                copy(rot, 4, send3[rot].at[0, early], final[rot].at[pl.ds(8, 6)], m3),
+                copy(rot, 5, send4[rot].at[early], final[rot].at[pl.ds(16, 6)], m4),
+                copy(rot, 6, send3[rot].at[1, late], passing[rot].at[late], m3),
+                copy(rot, 7, send3[rot].at[0, late], final[rot].at[pl.ds(14, 2)], m3),
+                copy(rot, 8, send4[rot].at[late], final[rot].at[pl.ds(22, 2)], m4),
+                copy(rot, 9, passing[rot].at[early], final[rot].at[pl.ds(24, 6)], m4),
+                copy(rot, 10, passing[rot].at[late], final[rot].at[pl.ds(30, 2)], m4),
             ]
         )
     for rot in range(ROTS):
@@ -183,57 +258,78 @@
         own = factors.at[:, pl.ds(rot * PIECE, PIECE), :]
         local.append(pltpu.make_async_copy(own, row[rot].at[pl.ds(0, 6)], local_sem.at[rot]))
         local[rot].start()
-
-    columns = jnp.transpose(own_energy[...])
+    local.append(pltpu.make_async_copy(integrals, resident, local_sem.at[ROTS]))
+    local[ROTS].start()
+
+    fill_table(table, source, slot, partners)
+
+    first = (lax.axis_index("wide") * 8 + lax.axis_index("narrow")) * LMO
+    own_rows[...] = jnp.zeros_like(own_rows)
+    for i in range(LMO):
+        own_rows[i : i + 1, :] = pao_energy[pl.ds(first + i, 1), :] - lmo_energy[first + i]
+
+    def fetch(i, carry):
+        for k in range(PARTNERS):
+            listed = partners[k, first + i]
+            other_energy[i * PARTNERS + k] = pao_energy[pl.ds(listed, 1), :] - lmo_energy[listed]
+        return carry
+
+    lax.fori_loop(0, LMO, fetch, 0)
+    columns = jnp.transpose(own_rows[...])
+    for copying in local:
+        copying.wait()
     for i in range(LMO):
         energy[i] = jnp.broadcast_to(columns[:, i : i + 1], (PAO, PAO))
-        flipped[:, i * PAO : (i + 1) * PAO] = jnp.transpose(integrals[i])
+        flipped[:, i * PAO : (i + 1) * PAO] = jnp.transpose(resident[i])
 
     for rot in range(ROTS):
         copies[rot][0].wait_recv()
         copies[rot][2].start()
-
-    def gather(rot, receiver, put):
-        def body(slot, carry):
-            put(slot, row[rot][table[rot * 32 + receiver * 8 + slot]])
+    for rot in range(ROTS):
+        copies[rot][1].wait_recv()
+
+    def gather(rot, receiver, part):
+        start, stop, held = (0, 6, row[rot]) if part == 0 else (6, 8, last[rot])
+
+        def body(at, carry):
+            value = held[table[rot * 32 + receiver * 8 + at]]
+            if receiver < 2:
+                send3[rot][receiver, at] = value
+            elif receiver == 2:
+                send4[rot][at] = value
+            else:
+                final[rot][at] = value
             return carry
 
-        lax.fori_loop(0, 8, body, 0)
-
-    def put_into(ref, base):
-        def put(slot, value):
-            ref[base + slot] = value
-
-        return put
-
-    def put_send3(rot, which):
-        def put(slot, value):
-            send3[rot][which, slot] = value
-
-        return put
-
-    for rot in range(ROTS):
-        local[rot].wait()
-        copies[rot][1].wait_recv()
+        lax.fori_loop(start, stop, body, 0)
+
+    for receiver, kind in ((1, 3), (0, 4), (2, 5)):
+        for rot in range(ROTS):
+            gather(rot, receiver, 0)
+            copies[rot][kind].start()
+    for rot in range(ROTS):
         copies[rot][2].wait_recv()
-        gather(rot, 1, put_send3(rot, 1))
-        copies[rot][3].start()
-    for rot in range(ROTS):
-        gather(rot, 0, put_send3(rot, 0))
-        copies[rot][4].start()
-        gather(rot, 2, put_into(send4[rot], 0))
-        copies[rot][5].start()
-    for rot in range(ROTS):
-        gather(rot, 3, put_into(final[rot], 0))
+        gather(rot, 1, 1)
+        copies[rot][6].start()
+    for rot in range(ROTS):
+        for receiver, kind in ((0, 7), (2, 8)):
+            gather(rot, receiver, 1)
+            copies[rot][kind].start()
+    for rot in range(ROTS):
+        gather(rot, 3, 0)
+        gather(rot, 3, 1)
     for rot in range(ROTS):
         copies[rot][3].wait_recv()
-        copies[rot][6].start()
-    for rot in range(ROTS):
-        for kind in (4, 5, 6):
+        copies[rot][9].start()
+    for rot in range(ROTS):
+        copies[rot][6].wait_recv()
+        copies[rot][10].start()
+    for rot in range(ROTS):
+        for kind in (4, 5, 7, 8, 9, 10):
             copies[rot][kind].wait_recv()
 
     def one(i, carry):
-        mine = factors[i]
+        mine = jnp.concatenate([row[rot][i] for rot in range(ROTS)], axis=0)
         gathered = jnp.zeros((PAO, AUX), jnp.float32)
         for k in range(PARTNERS):
             pair = i * PARTNERS + k
@@ -260,23 +356,31 @@
     reduce_total(tile, *reduction)
 
     for rot in range(ROTS):
-        for kind in range(7):
+        for kind in range(11):
             copies[rot][kind].wait_send()
 
 
-def exchange_and_multiply(table, factors, integrals, own_energy, other_energy):
+def local(factors, integrals, pao_energy, lmo_energy, partners):
     vmem = pl.BlockSpec(memory_space=pltpu.VMEM)
+    smem = pl.BlockSpec(memory_space=pltpu.SMEM)
+    anywhere = pl.BlockSpec(memory_space=pl.ANY)
     piece = (PIECE, AUX)
     scratch = []
-    for shape in ((24,), (2, 8), (8,), (8,), (32,)):
+    for shape in ((18,), (6,), (2, 8), (8,), (8,), (32,)):
         scratch += [pltpu.VMEM(shape + piece, jnp.bfloat16) for _ in range(ROTS)]
     scratch += [
+        pltpu.SMEM((128 + ROTS * PAIRS,), jnp.int32),
+        pltpu.SMEM((PAIRS,), jnp.int32),
+        pltpu.SMEM((PAIRS,), jnp.int32),
+        pltpu.VMEM((LMO, PAO, AUX), jnp.bfloat16),
+        pltpu.VMEM((8, PAO), jnp.float32),
+        pltpu.VMEM((PAIRS, 1, PAO), jnp.float32),
         pltpu.VMEM((AUX, LMO * PAO), jnp.bfloat16),
         pltpu.VMEM((LMO * PAO, AUX), jnp.bfloat16),
         pltpu.VMEM((LMO, PAO, PAO), jnp.float32),
-        pltpu.SemaphoreType.DMA((ROTS,)),
-        pltpu.SemaphoreType.DMA((ROTS, 7)),
-        pltpu.SemaphoreType.DMA((ROTS, 7)),
+        pltpu.SemaphoreType.DMA((ROTS + 1,)),
+        pltpu.SemaphoreType.DMA((ROTS, 11)),
+        pltpu.SemaphoreType.DMA((ROTS, 11)),
         pltpu.VMEM((AUX, AUX), jnp.float32),
         pltpu.VMEM((4, ROWS, AUX), jnp.float32),
         pltpu.VMEM((4, ROWS, AUX), jnp.float32),
@@ -294,62 +398,13 @@
     return pl.pallas_call(
         kernel,
         out_shape=jax.ShapeDtypeStruct((HEIGHT, ROWS), jnp.float32),
-        in_specs=[pl.BlockSpec(memory_space=pltpu.SMEM), vmem, vmem, vmem, vmem],
+        in_specs=[smem, smem, anywhere, anywhere, vmem],
         out_specs=vmem,
         scratch_shapes=scratch,
         compiler_params=pltpu.CompilerParams(
             collective_id=0, has_side_effects=True, vmem_limit_bytes=60 * 2**20
         ),
-    )(table, factors, integrals, own_energy, other_energy)
-
-
-def make_table(column, wide_index):
-    relative = jnp.take(column, wide_index ^ jnp.arange(16, dtype=jnp.int32), axis=0)
-    source = (relative // (LMO * 8)) ^ wide_index
-    slot = relative % LMO
-    at = source[:, None, :] == jnp.arange(16, dtype=jnp.int32)[None, :, None]
-    low = jnp.min(jnp.where(at, slot[:, None, :], LMO - 1), axis=2)
-    high = jnp.max(jnp.where(at, slot[:, None, :], 0), axis=2)
-    wanted = jnp.stack([low, high], axis=-1).reshape(-1)
-    pick, base = [], []
-    for rot in range(ROTS):
-        m1, m2, m3, m4 = order(rot)
-        for receiver in (m3, m3 ^ m4, m4, 0):
-            for q in range(4):
-                sender = (m1 if q & 1 else 0) ^ (m2 if q & 2 else 0)
-                for k in range(2):
-                    pick.append((receiver * 16 + sender) * 2 + k)
-                    base.append(q * LMO)
-    sends = wanted[np.array(pick)] + np.array(base, np.int32)
-
-    mine, mine_slot = source[0], slot[0]
-    is_high = mine_slot == jnp.sum(jnp.where(at[0], high[0][:, None], 0), axis=0)
-    digit = {}
-    for low_mask, high_mask, part in ((1, 3, mine % 4), (4, 12, mine // 4)):
-        digit[low_mask] = ((part == 1) | (part == 2)).astype(jnp.int32)
-        digit[high_mask] = ((part == 3) | (part == 2)).astype(jnp.int32)
-    places = []
-    for rot in range(ROTS):
-        m1, m2, m3, m4 = order(rot)
-        group = digit[m3] + 2 * digit[m4]
-        places.append((group * 4 + digit[m1] + 2 * digit[m2]) * 2 + is_high.astype(jnp.int32))
-    return jnp.concatenate([sends] + places).astype(jnp.int32)
-
-
-def local(factors, integrals, pao_energy, lmo_energy, partners):
-    wide_index = lax.axis_index("wide")
-    narrow_index = lax.axis_index("narrow")
-    first_lmo = (wide_index * 8 + narrow_index) * LMO
-    column = lax.dynamic_index_in_dim(
-        partners.reshape(16, 8, PAIRS), narrow_index, 1, keepdims=False
-    )
-    table = make_table(column, wide_index)
-    listed = lax.dynamic_slice_in_dim(partners, first_lmo, LMO, 0).reshape(PAIRS)
-    shifted = pao_energy - lmo_energy[:, None]
-    own_energy = lax.dynamic_slice_in_dim(shifted, first_lmo, LMO, 0)
-    own_energy = jnp.pad(own_energy, ((0, 8 - LMO), (0, 0)))
-    other_energy = jnp.take(shifted, listed, axis=0).reshape(PAIRS, 1, PAO)
-    return exchange_and_multiply(table, factors, integrals, own_energy, other_energy)
+    )(partners.T, lmo_energy, factors, integrals, pao_energy)
 
 
 def solution(mesh):

time: 163 us -> 152 us (0.933)
  local copies, waits for them, and re-layouts: 7.48 us -> 1.35 us
  other arithmetic: 3.77 us -> 0 us
  Pallas kernels: 152 us -> 150 us
    gather x3 -> x0, local copies, waits for them, and re-layouts: 2.42 us -> none  [the longest x1 1.27 us: make_table(): sends = wanted[np.array(pick)] + np.array(base, np.int32)]
where the time goes in v3:
time: 152 us
  Pallas kernels  150 us (99%)
    pallas_call x1, Pallas kernels, local(): pl.pallas_call(kernel, out_shape=jax.ShapeDtypeStruct((HEIGHT, ROWS), jnp...  150 us

profile of v3, /device:TPU:1, one launch (start us, length us, event | category | flops | bytes accessed | tf_op | source)
XLA Modules:
  0.0 151.6 jit_solution(876102430767668862)
XLA Ops:
  0.0 150.2 %shard_map.55 = f32[48,96]{1,0:T(8,128)} custom-call(s32[4,768]{1,0:T(4,128)} %bitcast.1, f32[768]{0:T(1024)} %lmo_energy.1, bf16[6,256,768]{2,1,0:T(8,128)(2,1)} %factors.1, bf16[6,256,768]{2,1,0:T(8,128)(2,1)} %integrals.1, f32[768,256]{1,0:T(8,128)} %pao_energy.1), custom_call_target="tpu_custom_call" | custom-call | tf_op jit(solution)/shard_map/pallas_call | solution.py:398
  150.2 1.3 copy.7

commit v4 on v3

--- a/solution.py
+++ b/solution.py
@@ -213,8 +213,7 @@
     total = reduction[0]
 
     barrier = pltpu.get_barrier_semaphore()
-    greeted = [neighbour(mask) for mask in range(1, 16)]
-    greeted += [along_y(0, 1), along_y(1), along_y(3)]
+    greeted = [neighbour(mask) for mask in MASKS] + [along_y(0, 1), along_y(1), along_y(3)]
     for device in greeted:
         pl.semaphore_signal(barrier, inc=1, device_id=device, device_id_type=MESH)
     pl.semaphore_wait(barrier, len(greeted))
@@ -330,17 +329,25 @@
 
     def one(i, carry):
         mine = jnp.concatenate([row[rot][i] for rot in range(ROTS)], axis=0)
-        gathered = jnp.zeros((PAO, AUX), jnp.float32)
-        for k in range(PARTNERS):
-            pair = i * PARTNERS + k
-            other = jnp.concatenate(
-                [final[rot][table[128 + rot * PAIRS + pair]] for rot in range(ROTS)], axis=0
-            )
-            integral = lax.dot_general(
-                mine, other, (((1,), (1,)), ((), ())), preferred_element_type=jnp.float32
-            )
-            amplitude = (integral / (energy[i] + other_energy[pair])).astype(jnp.bfloat16)
-            gathered = gathered + jnp.dot(amplitude, other, preferred_element_type=jnp.float32)
+        others = jnp.concatenate(
+            [
+                final[rot][table[128 + rot * PAIRS + i * PARTNERS + k]]
+                for k in range(PARTNERS)
+                for rot in range(ROTS)
+            ],
+            axis=0,
+        )
+        integral = lax.dot_general(
+            mine, others, (((1,), (1,)), ((), ())), preferred_element_type=jnp.float32
+        )
+        amplitude = jnp.concatenate(
+            [
+                (integral[:, k * PAO : (k + 1) * PAO] / (energy[i] + other_energy[i * PARTNERS + k]))
+                for k in range(PARTNERS)
+            ],
+            axis=1,
+        ).astype(jnp.bfloat16)
+        gathered = jnp.dot(amplitude, others, preferred_element_type=jnp.float32)
         fitted[pl.ds(pl.multiple_of(i * PAO, PAO), PAO), :] = gathered.astype(jnp.bfloat16)
         return carry
 

time: 152 us -> 148 us (0.974)
  Pallas kernels: 150 us -> 146 us
    pallas_call x1, Pallas kernels: 150 us -> 146 us  [local(): pl.pallas_call(kernel, out_shape=jax.ShapeDtypeStruct((HEIGHT, ROWS), jnp...]
where the time goes in v4:
time: 148 us
  Pallas kernels  146 us (99%)
    pallas_call x1, Pallas kernels, local(): pl.pallas_call(kernel, out_shape=jax.ShapeDtypeStruct((HEIGHT, ROWS), jnp...  146 us

profile of v4, /device:TPU:1, one launch (start us, length us, event | category | flops | bytes accessed | tf_op | source)
XLA Modules:
  0.0 147.8 jit_solution(14374188687793584569)
XLA Ops:
  0.0 146.4 %shard_map.55 = f32[48,96]{1,0:T(8,128)} custom-call(s32[4,768]{1,0:T(4,128)} %bitcast.1, f32[768]{0:T(1024)} %lmo_energy.1, bf16[6,256,768]{2,1,0:T(8,128)(2,1)} %factors.1, bf16[6,256,768]{2,1,0:T(8,128)(2,1)} %integrals.1, f32[768,256]{1,0:T(8,128)} %pao_energy.1), custom_call_target="tpu_custom_call" | custom-call | tf_op jit(solution)/shard_map/pallas_call | solution.py:405
  146.4 1.3 copy.7

commit v5 on v4

--- a/solution.py
+++ b/solution.py
@@ -13,6 +13,7 @@
 AUX = 768
 ROWS = AUX // 8
 HEIGHT = AUX // 16
+CHUNKS = AUX // 2 // 128
 ROTS = 4
 PIECE = PAO // ROTS
 
@@ -46,7 +47,7 @@
 
 
 def reduce_total(
-    tile, total, core_in, summed, first_out, first_in, second_out, second_in, block, turned, tiles_in,
+    tile, total, core_in, summed, first_out, first_in, second_out, second_in, block, turned, outgoing, tiles_in,
     core_sem, y_sem, wide_sem,
 ):
     narrow, wide = lax.axis_index("narrow"), lax.axis_index("wide")
@@ -80,33 +81,41 @@
         steps[u].wait_recv()
         summed[u] = total[band(u, core), :] + core_in[u]
 
-    left, right = slice(0, AUX // 2), slice(AUX // 2, AUX)
-    plan = ((left, 1, 3, (1, 2)), (right, 3, 1, (3, 2)))
-    firsts, seconds = [], []
-    for h, (columns, near, far, sent) in enumerate(plan):
-        for slot, u in enumerate(sent):
-            first_out[h, slot] = summed[u, :, columns].astype(first_out.dtype)
-        firsts.append(
-            send(first_out.at[h], first_in.at[h], (y_sem.at[0, h], y_sem.at[1, h]), along_y(near))
-        )
-        firsts[h].start()
-    for h, (columns, near, far, sent) in enumerate(plan):
-        firsts[h].wait_recv()
-        passed = summed[far, :, columns] + first_in[h, 1].astype(jnp.float32)
-        second_out[h] = passed.astype(second_out.dtype)
-        seconds.append(
-            send(second_out.at[h], second_in.at[h], (y_sem.at[2, h], y_sem.at[3, h]), along_y(far))
-        )
-        seconds[h].start()
+    plan = ((1, 3, (1, 2)), (3, 1, (3, 2)))
+    firsts, seconds = {}, {}
+    chunks = [(h, chunk) for chunk in range(CHUNKS) for h in range(2)]
+
+    def columns(h, chunk):
+        start = h * (AUX // 2) + chunk * 128
+        return slice(start, start + 128)
+
+    for h, chunk in chunks:
+        near, far, sent = plan[h]
+        for place, u in enumerate(sent):
+            first_out[h, chunk, place] = summed[u, :, columns(h, chunk)].astype(first_out.dtype)
+        firsts[h, chunk] = send(
+            first_out.at[h, chunk], first_in.at[h, chunk],
+            (y_sem.at[0, h, chunk], y_sem.at[1, h, chunk]), along_y(near),
+        )
+        firsts[h, chunk].start()
     block[pl.ds(ROWS, 128 - ROWS), :] = jnp.zeros((128 - ROWS, AUX), jnp.float32)
-    for h, (columns, near, far, sent) in enumerate(plan):
-        kept = summed[0, :, columns] + first_in[h, 0].astype(jnp.float32)
-        seconds[h].wait_recv()
-        block[pl.ds(0, ROWS), columns] = kept + second_in[h].astype(jnp.float32)
-
-    for j in range(AUX // 128):
-        at = slice(j * 128, j * 128 + 128)
+    for h, chunk in chunks:
+        near, far, sent = plan[h]
+        firsts[h, chunk].wait_recv()
+        passed = summed[far, :, columns(h, chunk)] + first_in[h, chunk, 1].astype(jnp.float32)
+        second_out[h, chunk] = passed.astype(second_out.dtype)
+        seconds[h, chunk] = send(
+            second_out.at[h, chunk], second_in.at[h, chunk],
+            (y_sem.at[2, h, chunk], y_sem.at[3, h, chunk]), along_y(far),
+        )
+        seconds[h, chunk].start()
+    for h, chunk in chunks:
+        at = columns(h, chunk)
+        kept = summed[0, :, at] + first_in[h, chunk, 0].astype(jnp.float32)
+        seconds[h, chunk].wait_recv()
+        block[pl.ds(0, ROWS), at] = kept + second_in[h, chunk].astype(jnp.float32)
         turned[at, :] = jnp.transpose(block[:, at])
+        outgoing[at, :] = turned[at, :].astype(outgoing.dtype)
 
     def rows(t):
         peer = flip(wide // 4, t // 4) * 4 + flip(lax.rem(wide, 4), t % 4)
@@ -115,17 +124,17 @@
     spread = []
     for t in range(1, 16):
         spread.append(
-            send(turned.at[rows(t)], tiles_in.at[t - 1],
+            send(outgoing.at[rows(t)], tiles_in.at[t - 1],
                  (wide_sem.at[0, t - 1], wide_sem.at[1, t - 1]), neighbour(t))
         )
         spread[-1].start()
     result = turned[rows(0), :]
     for t in range(1, 16):
         spread[t - 1].wait_recv()
-        result = result + tiles_in[t - 1]
+        result = result + tiles_in[t - 1].astype(jnp.float32)
     tile[...] = result[:, :ROWS]
 
-    for step in steps + firsts + seconds + spread:
+    for step in steps + list(firsts.values()) + list(seconds.values()) + spread:
         step.wait_send()
 
 
@@ -391,15 +400,16 @@
         pltpu.VMEM((AUX, AUX), jnp.float32),
         pltpu.VMEM((4, ROWS, AUX), jnp.float32),
         pltpu.VMEM((4, ROWS, AUX), jnp.float32),
-        pltpu.VMEM((2, 2, ROWS, AUX // 2), jnp.bfloat16),
-        pltpu.VMEM((2, 2, ROWS, AUX // 2), jnp.bfloat16),
-        pltpu.VMEM((2, ROWS, AUX // 2), jnp.bfloat16),
-        pltpu.VMEM((2, ROWS, AUX // 2), jnp.bfloat16),
+        pltpu.VMEM((2, CHUNKS, 2, ROWS, 128), jnp.bfloat16),
+        pltpu.VMEM((2, CHUNKS, 2, ROWS, 128), jnp.bfloat16),
+        pltpu.VMEM((2, CHUNKS, ROWS, 128), jnp.bfloat16),
+        pltpu.VMEM((2, CHUNKS, ROWS, 128), jnp.bfloat16),
         pltpu.VMEM((128, AUX), jnp.float32),
         pltpu.VMEM((AUX, 128), jnp.float32),
-        pltpu.VMEM((15, HEIGHT, 128), jnp.float32),
+        pltpu.VMEM((AUX, 128), jnp.bfloat16),
+        pltpu.VMEM((15, HEIGHT, 128), jnp.bfloat16),
         pltpu.SemaphoreType.DMA((2, 4)),
-        pltpu.SemaphoreType.DMA((4, 2)),
+        pltpu.SemaphoreType.DMA((4, 2, CHUNKS)),
         pltpu.SemaphoreType.DMA((2, 15)),
     ]
     return pl.pallas_call(

time: 148 us -> 145 us (0.980)
  Pallas kernels: 146 us -> 144 us
    pallas_call x1, Pallas kernels: 146 us -> 144 us  [local(): pl.pallas_call(kernel, out_shape=jax.ShapeDtypeStruct((HEIGHT, ROWS), jnp...]
where the time goes in v5:
time: 145 us
  Pallas kernels  144 us (99%)
    pallas_call x1, Pallas kernels, local(): pl.pallas_call(kernel, out_shape=jax.ShapeDtypeStruct((HEIGHT, ROWS), jnp...  144 us

profile of v5, /device:TPU:1, one launch (start us, length us, event | category | flops | bytes accessed | tf_op | source)
XLA Modules:
  0.0 145.3 jit_solution(3783599015266148893)
XLA Ops:
  0.0 143.9 %shard_map.55 = f32[48,96]{1,0:T(8,128)} custom-call(s32[4,768]{1,0:T(4,128)} %bitcast.1, f32[768]{0:T(1024)} %lmo_energy.1, bf16[6,256,768]{2,1,0:T(8,128)(2,1)} %factors.1, bf16[6,256,768]{2,1,0:T(8,128)(2,1)} %integrals.1, f32[768,256]{1,0:T(8,128)} %pao_energy.1), custom_call_target="tpu_custom_call" | custom-call | tf_op jit(solution)/shard_map/pallas_call | solution.py:415
  143.9 1.3 copy.7

commit v6 on v5

--- a/solution.py
+++ b/solution.py
@@ -16,6 +16,11 @@
 CHUNKS = AUX // 2 // 128
 ROTS = 4
 PIECE = PAO // ROTS
+ONCE = 8
+
+AT_ONCE = 128 + ROTS * PAIRS
+AT_RANK = AT_ONCE + PAIRS
+AT_LIST = AT_RANK + PAIRS
 
 MASKS = (1, 4, 3, 12)
 
@@ -47,7 +52,7 @@
 
 
 def reduce_total(
-    tile, total, core_in, summed, first_out, first_in, second_out, second_in, block, turned, outgoing, tiles_in,
+    tile, flipped, fitted, total, core_in, summed, first_out, first_in, second_out, second_in, block, turned, outgoing, tiles_in,
     core_sem, y_sem, wide_sem,
 ):
     narrow, wide = lax.axis_index("narrow"), lax.axis_index("wide")
@@ -59,27 +64,43 @@
             device_id=device, device_id_type=MESH,
         )
 
-    for i in range(3):
+    def multiply(i, j):
+        rows, columns = slice(i * 256, i * 256 + 256), slice(j * 256, j * 256 + 256)
+        total[rows, columns] = jnp.dot(
+            flipped[rows, :],
+            fitted[:, :, columns].reshape(LMO * PAO, 256),
+            preferred_element_type=jnp.float32,
+        )
+
+    def symmetrise(i, j):
+        at_i, at_j = slice(i * 256, i * 256 + 256), slice(j * 256, j * 256 + 256)
+        half = 0.5 * (total[at_i, at_j] + jnp.transpose(total[at_j, at_i]))
+        total[at_i, at_j] = half
+        if i != j:
+            total[at_j, at_i] = jnp.transpose(half)
+
+    def band(place, c):
+        return pl.ds(pl.multiple_of((place * 2 + c) * ROWS, ROWS), ROWS)
+
+    steps = []
+    for i, ready in enumerate(((0,), (1,), (2, 3))):
         for j in range(i, 3):
-            at_i, at_j = slice(i * 256, i * 256 + 256), slice(j * 256, j * 256 + 256)
-            half = 0.5 * (total[at_i, at_j] + jnp.transpose(total[at_j, at_i]))
-            total[at_i, at_j] = half
+            multiply(i, j)
             if i != j:
-                total[at_j, at_i] = jnp.transpose(half)
-
-    def band(u, c):
-        return pl.ds(pl.multiple_of((flip(y, u) * 2 + c) * ROWS, ROWS), ROWS)
-
-    steps = []
-    for u in range(4):
-        steps.append(
-            send(total.at[band(u, 1 - core)], core_in.at[u],
-                 (core_sem.at[0, u], core_sem.at[1, u]), along_y(0, 1))
-        )
-        steps[u].start()
+                multiply(j, i)
+        for j in range(i, 3):
+            symmetrise(i, j)
+        for place in ready:
+            steps.append(
+                send(total.at[band(place, 1 - core)], core_in.at[place],
+                     (core_sem.at[0, place], core_sem.at[1, place]), along_y(0, 1))
+            )
+            steps[-1].start()
+    for step in steps:
+        step.wait_recv()
     for u in (1, 2, 3, 0):
-        steps[u].wait_recv()
-        summed[u] = total[band(u, core), :] + core_in[u]
+        place = flip(y, u)
+        summed[u] = total[band(place, core), :] + core_in[place]
 
     plan = ((1, 3, (1, 2)), (3, 1, (3, 2)))
     firsts, seconds = {}, {}
@@ -160,16 +181,19 @@
                     holder = lax.div(owner, 8)
                     for q in range(4):
                         hit = holder == senders[q]
-                        low, high = found[2 * q], found[2 * q + 1]
-                        found[2 * q] = jnp.where(hit, jnp.minimum(low, place), low)
-                        found[2 * q + 1] = jnp.where(hit, jnp.maximum(high, place), high)
+                        low, high, summed = found[3 * q : 3 * q + 3]
+                        found[3 * q] = jnp.where(hit, jnp.minimum(low, place), low)
+                        found[3 * q + 1] = jnp.where(hit, jnp.maximum(high, place), high)
+                        found[3 * q + 2] = jnp.where(hit, summed + place, summed)
                 return tuple(found)
 
-            found = lax.fori_loop(0, LMO, scan, (jnp.int32(LMO - 1), jnp.int32(0)) * 4)
+            found = lax.fori_loop(0, LMO, scan, (jnp.int32(LMO - 1), jnp.int32(0), jnp.int32(0)) * 4)
             for q in range(4):
-                for k in range(2):
-                    base = q * LMO if q < 3 else 0
-                    table[rot * 32 + receiver * 8 + q * 2 + k] = found[2 * q + k] + base
+                low, high, summed = found[3 * q : 3 * q + 3]
+                twice = summed - low - high
+                for k, chosen in enumerate((twice, low + high - twice)):
+                    chosen = jnp.minimum(jnp.maximum(chosen, 0), LMO - 1)
+                    table[rot * 32 + receiver * 8 + k * 4 + q] = chosen + (q * LMO if q < 3 else 0)
 
     first = (wide * 8 + narrow) * LMO
 
@@ -186,14 +210,15 @@
     def place(pair, carry):
         mine, mine_slot = source[pair], slot[pair]
 
-        def larger(i, most):
+        def same(i, count):
             for k in range(PARTNERS):
-                there = slot[i * PARTNERS + k]
-                most = jnp.where(source[i * PARTNERS + k] == mine, jnp.maximum(most, there), most)
-            return most
-
-        most = lax.fori_loop(0, LMO, larger, jnp.int32(0))
-        is_high = jnp.where(mine_slot == most, 1, 0)
+                other = i * PARTNERS + k
+                count = jnp.where((source[other] == mine) & (slot[other] == mine_slot), count + 1, count)
+            return count
+
+        alone = lax.fori_loop(0, LMO, same, jnp.int32(0)) == 1
+        table[AT_ONCE + pair] = jnp.where(alone, 1, 0)
+        table[AT_RANK + pair] = jnp.where(alone, carry, ONCE)
         sz = lax.div(mine, 4)
         sx = mine - sz * 4
         digit = {}
@@ -203,10 +228,19 @@
         for rot in range(ROTS):
             m1, m2, m3, m4 = order(rot)
             block = (digit[m3] + 2 * digit[m4]) * 4 + digit[m1] + 2 * digit[m2]
-            table[128 + rot * PAIRS + pair] = block * 2 + is_high
-        return carry
-
-    lax.fori_loop(0, PAIRS, place, 0)
+            table[128 + rot * PAIRS + pair] = block
+        return jnp.where(alone, carry + 1, carry)
+
+    lax.fori_loop(0, PAIRS, place, jnp.int32(0))
+
+    def listed_once(rank, carry):
+        def find(pair, chosen):
+            return jnp.where(table[AT_RANK + pair] == rank, pair, chosen)
+
+        table[AT_LIST + rank] = lax.fori_loop(0, PAIRS, find, jnp.int32(0))
+        return carry
+
+    lax.fori_loop(0, ONCE, listed_once, 0)
 
 
 def kernel(partners, lmo_energy, factors, integrals, pao_energy, tile, *scratch):
@@ -215,11 +249,10 @@
     send3 = list(scratch[8:12])
     send4 = list(scratch[12:16])
     passing = list(scratch[16:20])
-    final = list(scratch[20:24])
-    (table, source, slot, resident, own_rows, other_energy, flipped, fitted, energy,
-     local_sem, send_sem, recv_sem) = scratch[24:36]
-    reduction = scratch[36:]
-    total = reduction[0]
+    final = [list(scratch[20:24]), list(scratch[24:28])]
+    (table, source, slot, own_rows, other_energy, flipped, fitted, energy, early_sum, product,
+     local_sem, send_sem, recv_sem) = scratch[28:41]
+    reduction = scratch[41:]
 
     barrier = pltpu.get_barrier_semaphore()
     greeted = [neighbour(mask) for mask in MASKS] + [along_y(0, 1), along_y(1), along_y(3)]
@@ -237,26 +270,25 @@
             device_id_type=MESH,
         )
 
-    early, late = pl.ds(0, 6), pl.ds(6, 2)
     copies = []
     for rot in range(ROTS):
         m1, m2, m3, m4 = order(rot)
         own = factors.at[:, pl.ds(rot * PIECE, PIECE), :]
-        copies.append(
-            [
-                copy(rot, 0, own, row[rot].at[pl.ds(6, 6)], m1),
-                copy(rot, 1, own, row[rot].at[pl.ds(12, 6)], m2),
-                copy(rot, 2, row[rot].at[pl.ds(6, 6)], last[rot], m2),
-                copy(rot, 3, send3[rot].at[1, early], passing[rot].at[early], m3),
-                copy(rot, 4, send3[rot].at[0, early], final[rot].at[pl.ds(8, 6)], m3),
-                copy(rot, 5, send4[rot].at[early], final[rot].at[pl.ds(16, 6)], m4),
-                copy(rot, 6, send3[rot].at[1, late], passing[rot].at[late], m3),
-                copy(rot, 7, send3[rot].at[0, late], final[rot].at[pl.ds(14, 2)], m3),
-                copy(rot, 8, send4[rot].at[late], final[rot].at[pl.ds(22, 2)], m4),
-                copy(rot, 9, passing[rot].at[early], final[rot].at[pl.ds(24, 6)], m4),
-                copy(rot, 10, passing[rot].at[late], final[rot].at[pl.ds(30, 2)], m4),
+        row_copies = [
+            copy(rot, 0, own, row[rot].at[pl.ds(6, 6)], m1),
+            copy(rot, 1, own, row[rot].at[pl.ds(12, 6)], m2),
+            copy(rot, 2, row[rot].at[pl.ds(6, 6)], last[rot], m2),
+        ]
+        for k, first, count in ((0, 0, 3), (0, 3, 1), (1, 0, 4)):
+            at, kind = pl.ds(first, count), len(row_copies)
+            place = [pl.ds(4 * block + first, count) for block in range(4)]
+            row_copies += [
+                copy(rot, kind, send3[rot].at[k, 1, at], passing[rot].at[k, at], m3),
+                copy(rot, kind + 1, send3[rot].at[k, 0, at], final[k][rot].at[place[1]], m3),
+                copy(rot, kind + 2, send4[rot].at[k, at], final[k][rot].at[place[2]], m4),
+                copy(rot, kind + 3, passing[rot].at[k, at], final[k][rot].at[place[3]], m4),
             ]
-        )
+        copies.append(row_copies)
     for rot in range(ROTS):
         copies[rot][0].start()
     for rot in range(ROTS):
@@ -266,7 +298,7 @@
         own = factors.at[:, pl.ds(rot * PIECE, PIECE), :]
         local.append(pltpu.make_async_copy(own, row[rot].at[pl.ds(0, 6)], local_sem.at[rot]))
         local[rot].start()
-    local.append(pltpu.make_async_copy(integrals, resident, local_sem.at[ROTS]))
+    local.append(pltpu.make_async_copy(integrals, fitted, local_sem.at[ROTS]))
     local[ROTS].start()
 
     fill_table(table, source, slot, partners)
@@ -288,7 +320,7 @@
         copying.wait()
     for i in range(LMO):
         energy[i] = jnp.broadcast_to(columns[:, i : i + 1], (PAO, PAO))
-        flipped[:, i * PAO : (i + 1) * PAO] = jnp.transpose(resident[i])
+        flipped[:, i * PAO : (i + 1) * PAO] = jnp.transpose(fitted[i])
 
     for rot in range(ROTS):
         copies[rot][0].wait_recv()
@@ -296,51 +328,58 @@
     for rot in range(ROTS):
         copies[rot][1].wait_recv()
 
-    def gather(rot, receiver, part):
-        start, stop, held = (0, 6, row[rot]) if part == 0 else (6, 8, last[rot])
-
-        def body(at, carry):
-            value = held[table[rot * 32 + receiver * 8 + at]]
+    def gather(rot, receiver, k, start, stop):
+        held = row[rot] if start < 3 else last[rot]
+
+        def body(q, carry):
+            value = held[table[rot * 32 + receiver * 8 + k * 4 + q]]
             if receiver < 2:
-                send3[rot][receiver, at] = value
+                send3[rot][k, receiver, q] = value
             elif receiver == 2:
-                send4[rot][at] = value
+                send4[rot][k, q] = value
             else:
-                final[rot][at] = value
+                final[k][rot][q] = value
             return carry
 
         lax.fori_loop(start, stop, body, 0)
 
     for receiver, kind in ((1, 3), (0, 4), (2, 5)):
         for rot in range(ROTS):
-            gather(rot, receiver, 0)
+            gather(rot, receiver, 0, 0, 3)
             copies[rot][kind].start()
     for rot in range(ROTS):
         copies[rot][2].wait_recv()
-        gather(rot, 1, 1)
-        copies[rot][6].start()
-    for rot in range(ROTS):
-        for receiver, kind in ((0, 7), (2, 8)):
-            gather(rot, receiver, 1)
+        gather(rot, 1, 0, 3, 4)
+        copies[rot][7].start()
+    for rot in range(ROTS):
+        for receiver, kind in ((0, 8), (2, 9)):
+            gather(rot, receiver, 0, 3, 4)
             copies[rot][kind].start()
     for rot in range(ROTS):
-        gather(rot, 3, 0)
-        gather(rot, 3, 1)
-    for rot in range(ROTS):
-        copies[rot][3].wait_recv()
-        copies[rot][9].start()
-    for rot in range(ROTS):
-        copies[rot][6].wait_recv()
-        copies[rot][10].start()
-    for rot in range(ROTS):
-        for kind in (4, 5, 7, 8, 9, 10):
+        for receiver in (1, 0, 2):
+            gather(rot, receiver, 1, 0, 3)
+            gather(rot, receiver, 1, 3, 4)
+    for kind in (3, 7):
+        for rot in range(ROTS):
+            copies[rot][kind].wait_recv()
+            copies[rot][kind + 3].start()
+    for kind in (11, 12, 13):
+        for rot in range(ROTS):
+            copies[rot][kind].start()
+    for rot in range(ROTS):
+        for k in range(2):
+            gather(rot, 3, k, 0, 3)
+            gather(rot, 3, k, 3, 4)
+    product[ONCE] = jnp.zeros((PAO, AUX), jnp.float32)
+    for rot in range(ROTS):
+        for kind in (4, 5, 6, 8, 9, 10):
             copies[rot][kind].wait_recv()
 
     def one(i, carry):
         mine = jnp.concatenate([row[rot][i] for rot in range(ROTS)], axis=0)
         others = jnp.concatenate(
             [
-                final[rot][table[128 + rot * PAIRS + i * PARTNERS + k]]
+                final[0][rot][table[128 + rot * PAIRS + i * PARTNERS + k]]
                 for k in range(PARTNERS)
                 for rot in range(ROTS)
             ],
@@ -349,30 +388,57 @@
         integral = lax.dot_general(
             mine, others, (((1,), (1,)), ((), ())), preferred_element_type=jnp.float32
         )
-        amplitude = jnp.concatenate(
-            [
-                (integral[:, k * PAO : (k + 1) * PAO] / (energy[i] + other_energy[i * PARTNERS + k]))
-                for k in range(PARTNERS)
-            ],
-            axis=1,
-        ).astype(jnp.bfloat16)
-        gathered = jnp.dot(amplitude, others, preferred_element_type=jnp.float32)
-        fitted[pl.ds(pl.multiple_of(i * PAO, PAO), PAO), :] = gathered.astype(jnp.bfloat16)
-        return carry
-
-    lax.fori_loop(0, LMO, one, 0)
-
-    def rows(block, carry):
-        at = pl.ds(pl.multiple_of(block * 256, 256), 256)
-        total[at, :] = jnp.dot(flipped[at, :], fitted[...], preferred_element_type=jnp.float32)
-        return carry
-
-    lax.fori_loop(0, AUX // 256, rows, 0)
-
-    reduce_total(tile, *reduction)
-
-    for rot in range(ROTS):
-        for kind in range(11):
+        parts = []
+        for k in range(PARTNERS):
+            pair = i * PARTNERS + k
+            keep = jnp.where(table[AT_ONCE + pair] == 1, 0.0, 1.0)
+            parts.append(
+                integral[:, k * PAO : (k + 1) * PAO] / (energy[i] + other_energy[pair]) * keep
+            )
+        amplitude = jnp.concatenate(parts, axis=1).astype(jnp.bfloat16)
+        early_sum[i] = jnp.dot(amplitude, others, preferred_element_type=jnp.float32)
+        return carry
+
+    lax.fori_loop(0, LMO // 2, one, 0)
+    for rot in range(ROTS):
+        copies[rot][11].wait_recv()
+        copies[rot][14].start()
+    lax.fori_loop(LMO // 2, LMO, one, 0)
+    for rot in range(ROTS):
+        for kind in (12, 13, 14):
+            copies[rot][kind].wait_recv()
+
+    def remaining(step, carry):
+        for part in range(4):
+            rank = step * 4 + part
+            pair = table[AT_LIST + rank]
+            i = lax.div(pair, PARTNERS)
+            mine = jnp.concatenate([row[rot][i] for rot in range(ROTS)], axis=0)
+            other = jnp.concatenate(
+                [final[1][rot][table[128 + rot * PAIRS + pair]] for rot in range(ROTS)], axis=0
+            )
+            integral = lax.dot_general(
+                mine, other, (((1,), (1,)), ((), ())), preferred_element_type=jnp.float32
+            )
+            amplitude = (integral / (energy[i] + other_energy[pair])).astype(jnp.bfloat16)
+            product[rank] = jnp.dot(amplitude, other, preferred_element_type=jnp.float32)
+        return carry
+
+    lax.fori_loop(0, ONCE // 4, remaining, 0)
+
+    def combine(i, carry):
+        gathered = early_sum[i]
+        for k in range(PARTNERS):
+            gathered = gathered + product[table[AT_RANK + i * PARTNERS + k]]
+        fitted[i] = gathered.astype(jnp.bfloat16)
+        return carry
+
+    lax.fori_loop(0, LMO, combine, 0)
+
+    reduce_total(tile, flipped, fitted, *reduction)
+
+    for rot in range(ROTS):
+        for kind in range(15):
             copies[rot][kind].wait_send()
 
 
@@ -382,21 +448,22 @@
     anywhere = pl.BlockSpec(memory_space=pl.ANY)
     piece = (PIECE, AUX)
     scratch = []
-    for shape in ((18,), (6,), (2, 8), (8,), (8,), (32,)):
+    for shape in ((18,), (6,), (2, 2, 4), (2, 4), (2, 4), (16,), (16,)):
         scratch += [pltpu.VMEM(shape + piece, jnp.bfloat16) for _ in range(ROTS)]
     scratch += [
-        pltpu.SMEM((128 + ROTS * PAIRS,), jnp.int32),
+        pltpu.SMEM((AT_LIST + ONCE,), jnp.int32),
         pltpu.SMEM((PAIRS,), jnp.int32),
         pltpu.SMEM((PAIRS,), jnp.int32),
-        pltpu.VMEM((LMO, PAO, AUX), jnp.bfloat16),
         pltpu.VMEM((8, PAO), jnp.float32),
         pltpu.VMEM((PAIRS, 1, PAO), jnp.float32),
         pltpu.VMEM((AUX, LMO * PAO), jnp.bfloat16),
-        pltpu.VMEM((LMO * PAO, AUX), jnp.bfloat16),
+        pltpu.VMEM((LMO, PAO, AUX), jnp.bfloat16),
         pltpu.VMEM((LMO, PAO, PAO), jnp.float32),
+        pltpu.VMEM((LMO, PAO, AUX), jnp.float32),
+        pltpu.VMEM((ONCE + 1, PAO, AUX), jnp.float32),
         pltpu.SemaphoreType.DMA((ROTS + 1,)),
-        pltpu.SemaphoreType.DMA((ROTS, 11)),
-        pltpu.SemaphoreType.DMA((ROTS, 11)),
+        pltpu.SemaphoreType.DMA((ROTS, 15)),
+        pltpu.SemaphoreType.DMA((ROTS, 15)),
         pltpu.VMEM((AUX, AUX), jnp.float32),
         pltpu.VMEM((4, ROWS, AUX), jnp.float32),
         pltpu.VMEM((4, ROWS, AUX), jnp.float32),

time: 145 us -> 142 us (0.979)
  Pallas kernels: 144 us -> 141 us
    pallas_call x1, Pallas kernels: 144 us -> 141 us  [local(): pl.pallas_call(kernel, out_shape=jax.ShapeDtypeStruct((HEIGHT, ROWS), jnp...]
where the time goes in v6:
time: 142 us
  Pallas kernels  141 us (99%)
    pallas_call x1, Pallas kernels, local(): pl.pallas_call(kernel, out_shape=jax.ShapeDtypeStruct((HEIGHT, ROWS), jnp...  141 us

profile of v6, /device:TPU:1, one launch (start us, length us, event | category | flops | bytes accessed | tf_op | source)
XLA Modules:
  0.0 142.0 jit_solution(13879705950581762394)
XLA Ops:
  0.0 140.7 %shard_map.55 = f32[48,96]{1,0:T(8,128)} custom-call(s32[4,768]{1,0:T(4,128)} %bitcast.1, f32[768]{0:T(1024)} %lmo_energy.1, bf16[6,256,768]{2,1,0:T(8,128)(2,1)} %factors.1, bf16[6,256,768]{2,1,0:T(8,128)(2,1)} %integrals.1, f32[768,256]{1,0:T(8,128)} %pao_energy.1), custom_call_target="tpu_custom_call" | custom-call | tf_op jit(solution)/shard_map/pallas_call | solution.py:482
  140.7 1.3 copy.7

commit v7 on v6

--- a/solution.py
+++ b/solution.py
@@ -66,7 +66,7 @@
 
     def multiply(i, j):
         rows, columns = slice(i * 256, i * 256 + 256), slice(j * 256, j * 256 + 256)
-        total[rows, columns] = jnp.dot(
+        total[j, rows] = jnp.dot(
             flipped[rows, :],
             fitted[:, :, columns].reshape(LMO * PAO, 256),
             preferred_element_type=jnp.float32,
@@ -74,46 +74,47 @@
 
     def symmetrise(i, j):
         at_i, at_j = slice(i * 256, i * 256 + 256), slice(j * 256, j * 256 + 256)
-        half = 0.5 * (total[at_i, at_j] + jnp.transpose(total[at_j, at_i]))
-        total[at_i, at_j] = half
+        half = 0.5 * (total[j, at_i] + jnp.transpose(total[i, at_j]))
+        total[j, at_i] = half
         if i != j:
-            total[at_j, at_i] = jnp.transpose(half)
+            total[i, at_j] = jnp.transpose(half)
 
     def band(place, c):
         return pl.ds(pl.multiple_of((place * 2 + c) * ROWS, ROWS), ROWS)
 
     steps = []
-    for i, ready in enumerate(((0,), (1,), (2, 3))):
-        for j in range(i, 3):
+    for i in range(CHUNKS):
+        for j in range(i, CHUNKS):
             multiply(i, j)
             if i != j:
                 multiply(j, i)
-        for j in range(i, 3):
+        for j in range(i, CHUNKS):
             symmetrise(i, j)
-        for place in ready:
+        for place in range(4):
             steps.append(
-                send(total.at[band(place, 1 - core)], core_in.at[place],
-                     (core_sem.at[0, place], core_sem.at[1, place]), along_y(0, 1))
+                send(total.at[i, band(place, 1 - core)], core_in.at[i, place],
+                     (core_sem.at[0, i, place], core_sem.at[1, i, place]), along_y(0, 1))
             )
             steps[-1].start()
-    for step in steps:
-        step.wait_recv()
-    for u in (1, 2, 3, 0):
-        place = flip(y, u)
-        summed[u] = total[band(place, core), :] + core_in[place]
 
     plan = ((1, 3, (1, 2)), (3, 1, (3, 2)))
     firsts, seconds = {}, {}
     chunks = [(h, chunk) for chunk in range(CHUNKS) for h in range(2)]
 
     def columns(h, chunk):
-        start = h * (AUX // 2) + chunk * 128
+        start = chunk * 256 + h * 128
         return slice(start, start + 128)
 
     for h, chunk in chunks:
         near, far, sent = plan[h]
+        if h == 0:
+            for step in steps[4 * chunk : 4 * chunk + 4]:
+                step.wait_recv()
+            at = pl.ds(chunk * 256, 256)
+            for place in range(4):
+                summed[place, :, at] = total[chunk, band(place, core)] + core_in[chunk, place]
         for place, u in enumerate(sent):
-            first_out[h, chunk, place] = summed[u, :, columns(h, chunk)].astype(first_out.dtype)
+            first_out[h, chunk, place] = summed[flip(y, u), :, columns(h, chunk)].astype(first_out.dtype)
         firsts[h, chunk] = send(
             first_out.at[h, chunk], first_in.at[h, chunk],
             (y_sem.at[0, h, chunk], y_sem.at[1, h, chunk]), along_y(near),
@@ -123,7 +124,7 @@
     for h, chunk in chunks:
         near, far, sent = plan[h]
         firsts[h, chunk].wait_recv()
-        passed = summed[far, :, columns(h, chunk)] + first_in[h, chunk, 1].astype(jnp.float32)
+        passed = summed[flip(y, far), :, columns(h, chunk)] + first_in[h, chunk, 1].astype(jnp.float32)
         second_out[h, chunk] = passed.astype(second_out.dtype)
         seconds[h, chunk] = send(
             second_out.at[h, chunk], second_in.at[h, chunk],
@@ -132,7 +133,7 @@
         seconds[h, chunk].start()
     for h, chunk in chunks:
         at = columns(h, chunk)
-        kept = summed[0, :, at] + first_in[h, chunk, 0].astype(jnp.float32)
+        kept = summed[y, :, at] + first_in[h, chunk, 0].astype(jnp.float32)
         seconds[h, chunk].wait_recv()
         block[pl.ds(0, ROWS), at] = kept + second_in[h, chunk].astype(jnp.float32)
         turned[at, :] = jnp.transpose(block[:, at])
@@ -371,6 +372,11 @@
             gather(rot, 3, k, 0, 3)
             gather(rot, 3, k, 3, 4)
     product[ONCE] = jnp.zeros((PAO, AUX), jnp.float32)
+    total = reduction[0]
+    blocks = [(rank // 3, pl.ds(rank % 3 * PAO, PAO)) for rank in range(ONCE)]
+    for rank in range(ONCE):
+        pair = table[AT_LIST + rank]
+        total[blocks[rank]] = 1.0 / (energy[lax.div(pair, PARTNERS)] + other_energy[pair])
     for rot in range(ROTS):
         for kind in (4, 5, 6, 8, 9, 10):
             copies[rot][kind].wait_recv()
@@ -408,23 +414,18 @@
         for kind in (12, 13, 14):
             copies[rot][kind].wait_recv()
 
-    def remaining(step, carry):
-        for part in range(4):
-            rank = step * 4 + part
-            pair = table[AT_LIST + rank]
-            i = lax.div(pair, PARTNERS)
-            mine = jnp.concatenate([row[rot][i] for rot in range(ROTS)], axis=0)
-            other = jnp.concatenate(
-                [final[1][rot][table[128 + rot * PAIRS + pair]] for rot in range(ROTS)], axis=0
-            )
-            integral = lax.dot_general(
-                mine, other, (((1,), (1,)), ((), ())), preferred_element_type=jnp.float32
-            )
-            amplitude = (integral / (energy[i] + other_energy[pair])).astype(jnp.bfloat16)
-            product[rank] = jnp.dot(amplitude, other, preferred_element_type=jnp.float32)
-        return carry
-
-    lax.fori_loop(0, ONCE // 4, remaining, 0)
+    for rank in range(ONCE):
+        pair = table[AT_LIST + rank]
+        i = lax.div(pair, PARTNERS)
+        mine = jnp.concatenate([row[rot][i] for rot in range(ROTS)], axis=0)
+        other = jnp.concatenate(
+            [final[1][rot][table[128 + rot * PAIRS + pair]] for rot in range(ROTS)], axis=0
+        )
+        integral = lax.dot_general(
+            mine, other, (((1,), (1,)), ((), ())), preferred_element_type=jnp.float32
+        )
+        amplitude = (integral * total[blocks[rank]]).astype(jnp.bfloat16)
+        product[rank] = jnp.dot(amplitude, other, preferred_element_type=jnp.float32)
 
     def combine(i, carry):
         gathered = early_sum[i]
@@ -464,8 +465,8 @@
         pltpu.SemaphoreType.DMA((ROTS + 1,)),
         pltpu.SemaphoreType.DMA((ROTS, 15)),
         pltpu.SemaphoreType.DMA((ROTS, 15)),
-        pltpu.VMEM((AUX, AUX), jnp.float32),
-        pltpu.VMEM((4, ROWS, AUX), jnp.float32),
+        pltpu.VMEM((CHUNKS, AUX, 256), jnp.float32),
+        pltpu.VMEM((CHUNKS, 4, ROWS, 256), jnp.float32),
         pltpu.VMEM((4, ROWS, AUX), jnp.float32),
         pltpu.VMEM((2, CHUNKS, 2, ROWS, 128), jnp.bfloat16),
         pltpu.VMEM((2, CHUNKS, 2, ROWS, 128), jnp.bfloat16),
@@ -475,7 +476,7 @@
         pltpu.VMEM((AUX, 128), jnp.float32),
         pltpu.VMEM((AUX, 128), jnp.bfloat16),
         pltpu.VMEM((15, HEIGHT, 128), jnp.bfloat16),
-        pltpu.SemaphoreType.DMA((2, 4)),
+        pltpu.SemaphoreType.DMA((2, CHUNKS, 4)),
         pltpu.SemaphoreType.DMA((4, 2, CHUNKS)),
         pltpu.SemaphoreType.DMA((2, 15)),
     ]

time: 142 us -> 140 us (0.986)
  Pallas kernels: 141 us -> 138 us
    pallas_call x1, Pallas kernels: 141 us -> 138 us  [local(): pl.pallas_call(kernel, out_shape=jax.ShapeDtypeStruct((HEIGHT, ROWS), jnp...]
where the time goes in v7:
time: 140 us
  Pallas kernels  138 us (99%)
    pallas_call x1, Pallas kernels, local(): pl.pallas_call(kernel, out_shape=jax.ShapeDtypeStruct((HEIGHT, ROWS), jnp...  138 us

profile of v7, /device:TPU:1, one launch (start us, length us, event | category | flops | bytes accessed | tf_op | source)
XLA Modules:
  0.0 139.5 jit_solution(5191126057981338937)
XLA Ops:
  0.0 138.2 %shard_map.55 = f32[48,96]{1,0:T(8,128)} custom-call(s32[4,768]{1,0:T(4,128)} %bitcast.1, f32[768]{0:T(1024)} %lmo_energy.1, bf16[6,256,768]{2,1,0:T(8,128)(2,1)} %factors.1, bf16[6,256,768]{2,1,0:T(8,128)(2,1)} %integrals.1, f32[768,256]{1,0:T(8,128)} %pao_energy.1), custom_call_target="tpu_custom_call" | custom-call | tf_op jit(solution)/shard_map/pallas_call | solution.py:483
  138.2 1.3 copy.7

commit v8 on v7

--- a/solution.py
+++ b/solution.py
@@ -131,6 +131,28 @@
             (y_sem.at[2, h, chunk], y_sem.at[3, h, chunk]), along_y(far),
         )
         seconds[h, chunk].start()
+    def row_of(t):
+        peer = flip(wide // 4, t // 4) * 4 + flip(lax.rem(wide, 4), t % 4)
+        return peer * HEIGHT
+
+    def rows(t):
+        return pl.ds(pl.multiple_of(row_of(t), HEIGHT), HEIGHT)
+
+    spread = []
+    for t in range(1, 16):
+        spread.append(
+            send(outgoing.at[rows(t)], tiles_in.at[t - 1],
+                 (wide_sem.at[0, t - 1], wide_sem.at[1, t - 1]), neighbour(t))
+        )
+
+    def send_tiles(chunk):
+        for t in range(1, 16):
+            end = row_of(t) + HEIGHT
+
+            @pl.when((end > chunk * 256) & (end <= chunk * 256 + 256))
+            def _():
+                spread[t - 1].start()
+
     for h, chunk in chunks:
         at = columns(h, chunk)
         kept = summed[y, :, at] + first_in[h, chunk, 0].astype(jnp.float32)
@@ -138,18 +160,9 @@
         block[pl.ds(0, ROWS), at] = kept + second_in[h, chunk].astype(jnp.float32)
         turned[at, :] = jnp.transpose(block[:, at])
         outgoing[at, :] = turned[at, :].astype(outgoing.dtype)
-
-    def rows(t):
-        peer = flip(wide // 4, t // 4) * 4 + flip(lax.rem(wide, 4), t % 4)
-        return pl.ds(pl.multiple_of(peer * HEIGHT, HEIGHT), HEIGHT)
-
-    spread = []
-    for t in range(1, 16):
-        spread.append(
-            send(outgoing.at[rows(t)], tiles_in.at[t - 1],
-                 (wide_sem.at[0, t - 1], wide_sem.at[1, t - 1]), neighbour(t))
-        )
-        spread[-1].start()
+        if h == 1:
+            send_tiles(chunk)
+
     result = turned[rows(0), :]
     for t in range(1, 16):
         spread[t - 1].wait_recv()

time: 140 us -> 138 us (0.986)
  Pallas kernels: 138 us -> 136 us
    pallas_call x1, Pallas kernels: 138 us -> 136 us  [local(): pl.pallas_call(kernel, out_shape=jax.ShapeDtypeStruct((HEIGHT, ROWS), jnp...]
where the time goes in v8:
time: 138 us; the launch traced here: 137 us
  Pallas kernels  136 us (99%)
    pallas_call x1, Pallas kernels, local(): pl.pallas_call(kernel, out_shape=jax.ShapeDtypeStruct((HEIGHT, ROWS), jnp...  136 us

profile of v8, /device:TPU:1, one launch (start us, length us, event | category | flops | bytes accessed | tf_op | source)
XLA Modules:
  0.0 137.4 jit_solution(12845487890489748820)
XLA Ops:
  0.0 136.0 %shard_map.55 = f32[48,96]{1,0:T(8,128)} custom-call(s32[4,768]{1,0:T(4,128)} %bitcast.1, f32[768]{0:T(1024)} %lmo_energy.1, bf16[6,256,768]{2,1,0:T(8,128)(2,1)} %factors.1, bf16[6,256,768]{2,1,0:T(8,128)(2,1)} %integrals.1, f32[768,256]{1,0:T(8,128)} %pao_energy.1), custom_call_target="tpu_custom_call" | custom-call | tf_op jit(solution)/shard_map/pallas_call | solution.py:496
  136.0 1.3 copy.7

commit v9 on v8

--- a/solution.py
+++ b/solution.py
@@ -7,6 +7,7 @@
 
 MESH = pl.DeviceIdType.MESH
 LMO = 6
+LMOS = 768
 PARTNERS = 4
 PAIRS = LMO * PARTNERS
 PAO = 256
@@ -257,7 +258,7 @@
     lax.fori_loop(0, ONCE, listed_once, 0)
 
 
-def kernel(partners, lmo_energy, factors, integrals, pao_energy, tile, *scratch):
+def kernel(partners_in, lmo_energy_in, factors, integrals, pao_energy_in, tile, *scratch):
     row = list(scratch[0:4])
     last = list(scratch[4:8])
     send3 = list(scratch[8:12])
@@ -265,8 +266,8 @@
     passing = list(scratch[16:20])
     final = [list(scratch[20:24]), list(scratch[24:28])]
     (table, source, slot, own_rows, other_energy, flipped, fitted, energy, early_sum, product,
-     local_sem, send_sem, recv_sem) = scratch[28:41]
-    reduction = scratch[41:]
+     partners, lmo_energy, pao_energy, local_sem, send_sem, recv_sem) = scratch[28:44]
+    reduction = scratch[44:]
 
     barrier = pltpu.get_barrier_semaphore()
     greeted = [neighbour(mask) for mask in MASKS] + [along_y(0, 1), along_y(1), along_y(3)]
@@ -307,6 +308,12 @@
         copies[rot][0].start()
     for rot in range(ROTS):
         copies[rot][1].start()
+    small = []
+    for item, (src, dst) in enumerate(
+        ((partners_in, partners), (lmo_energy_in, lmo_energy), (pao_energy_in, pao_energy))
+    ):
+        small.append(pltpu.make_async_copy(src, dst, local_sem.at[ROTS + 1 + item]))
+        small[item].start()
     local = []
     for rot in range(ROTS):
         own = factors.at[:, pl.ds(rot * PIECE, PIECE), :]
@@ -315,6 +322,8 @@
     local.append(pltpu.make_async_copy(integrals, fitted, local_sem.at[ROTS]))
     local[ROTS].start()
 
+    for copying in small:
+        copying.wait()
     fill_table(table, source, slot, partners)
 
     first = (lax.axis_index("wide") * 8 + lax.axis_index("narrow")) * LMO
@@ -458,7 +467,6 @@
 
 def local(factors, integrals, pao_energy, lmo_energy, partners):
     vmem = pl.BlockSpec(memory_space=pltpu.VMEM)
-    smem = pl.BlockSpec(memory_space=pltpu.SMEM)
     anywhere = pl.BlockSpec(memory_space=pl.ANY)
     piece = (PIECE, AUX)
     scratch = []
@@ -475,7 +483,10 @@
         pltpu.VMEM((LMO, PAO, PAO), jnp.float32),
         pltpu.VMEM((LMO, PAO, AUX), jnp.float32),
         pltpu.VMEM((ONCE + 1, PAO, AUX), jnp.float32),
-        pltpu.SemaphoreType.DMA((ROTS + 1,)),
+        pltpu.SMEM((PARTNERS, LMOS), jnp.int32),
+        pltpu.SMEM((LMOS,), jnp.float32),
+        pltpu.VMEM((LMOS, PAO), jnp.float32),
+        pltpu.SemaphoreType.DMA((ROTS + 4,)),
         pltpu.SemaphoreType.DMA((ROTS, 15)),
         pltpu.SemaphoreType.DMA((ROTS, 15)),
         pltpu.VMEM((CHUNKS, AUX, 256), jnp.float32),
@@ -496,7 +507,7 @@
     return pl.pallas_call(
         kernel,
         out_shape=jax.ShapeDtypeStruct((HEIGHT, ROWS), jnp.float32),
-        in_specs=[smem, smem, anywhere, anywhere, vmem],
+        in_specs=[anywhere] * 5,
         out_specs=vmem,
         scratch_shapes=scratch,
         compiler_params=pltpu.CompilerParams(

time: 138 us -> 137 us (level)
  no operation moved by 1% of the time
where the time goes in v9:
time: 137 us; the launch traced here: 136 us
  Pallas kernels  135 us (99%)
    pallas_call x1, Pallas kernels, local(): pl.pallas_call(kernel, out_shape=jax.ShapeDtypeStruct((HEIGHT, ROWS), jnp...  135 us

profile of v9, /device:TPU:1, one launch (start us, length us, event | category | flops | bytes accessed | tf_op | source)
XLA Modules:
  0.0 136.2 jit_solution(12329160150391355171)
XLA Ops:
  0.0 134.9 %shard_map.55 = f32[48,96]{1,0:T(8,128)} custom-call(s32[4,768]{1,0:T(4,128)} %bitcast.1, f32[768]{0:T(1024)} %lmo_energy_in.1, bf16[6,256,768]{2,1,0:T(8,128)(2,1)} %factors.1, bf16[6,256,768]{2,1,0:T(8,128)(2,1)} %integrals.1, f32[768,256]{1,0:T(8,128)} %pao_energy_in.1), custom_call_target="tpu_custom_call" | custom-call | tf_op jit(solution)/shard_map/pallas_call | solution.py:507
  134.9 1.3 copy.7

commit v10 on v9

--- a/solution.py
+++ b/solution.py
@@ -53,7 +53,7 @@
 
 
 def reduce_total(
-    tile, flipped, fitted, total, core_in, summed, first_out, first_in, second_out, second_in, block, turned, outgoing, tiles_in,
+    sent, tile, flipped, fitted, total, core_in, summed, first_out, first_in, second_out, second_in, block, turned, outgoing, tiles_in,
     core_sem, y_sem, wide_sem,
 ):
     narrow, wide = lax.axis_index("narrow"), lax.axis_index("wide")
@@ -107,14 +107,14 @@
         return slice(start, start + 128)
 
     for h, chunk in chunks:
-        near, far, sent = plan[h]
+        near, far, leaving = plan[h]
         if h == 0:
             for step in steps[4 * chunk : 4 * chunk + 4]:
                 step.wait_recv()
             at = pl.ds(chunk * 256, 256)
             for place in range(4):
                 summed[place, :, at] = total[chunk, band(place, core)] + core_in[chunk, place]
-        for place, u in enumerate(sent):
+        for place, u in enumerate(leaving):
             first_out[h, chunk, place] = summed[flip(y, u), :, columns(h, chunk)].astype(first_out.dtype)
         firsts[h, chunk] = send(
             first_out.at[h, chunk], first_in.at[h, chunk],
@@ -123,7 +123,7 @@
         firsts[h, chunk].start()
     block[pl.ds(ROWS, 128 - ROWS), :] = jnp.zeros((128 - ROWS, AUX), jnp.float32)
     for h, chunk in chunks:
-        near, far, sent = plan[h]
+        near, far, leaving = plan[h]
         firsts[h, chunk].wait_recv()
         passed = summed[flip(y, far), :, columns(h, chunk)] + first_in[h, chunk, 1].astype(jnp.float32)
         second_out[h, chunk] = passed.astype(second_out.dtype)
@@ -164,13 +164,15 @@
         if h == 1:
             send_tiles(chunk)
 
+    for step in sent + steps + list(firsts.values()) + list(seconds.values()):
+        step.wait_send()
     result = turned[rows(0), :]
     for t in range(1, 16):
         spread[t - 1].wait_recv()
         result = result + tiles_in[t - 1].astype(jnp.float32)
     tile[...] = result[:, :ROWS]
 
-    for step in steps + list(firsts.values()) + list(seconds.values()) + spread:
+    for step in spread:
         step.wait_send()
 
 
@@ -433,6 +435,9 @@
         copies[rot][14].start()
     lax.fori_loop(LMO // 2, LMO, one, 0)
     for rot in range(ROTS):
+        for kind in range(11):
+            copies[rot][kind].wait_send()
+    for rot in range(ROTS):
         for kind in (12, 13, 14):
             copies[rot][kind].wait_recv()
 
@@ -458,11 +463,8 @@
 
     lax.fori_loop(0, LMO, combine, 0)
 
-    reduce_total(tile, flipped, fitted, *reduction)
-
-    for rot in range(ROTS):
-        for kind in range(15):
-            copies[rot][kind].wait_send()
+    sent = [copies[rot][kind] for rot in range(ROTS) for kind in range(11, 15)]
+    reduce_total(sent, tile, flipped, fitted, *reduction)
 
 
 def local(factors, integrals, pao_energy, lmo_energy, partners):

time: 137 us -> 137 us (level)
  no operation moved by 1% of the time
where the time goes in v10:
time: 137 us; the launch traced here: 136 us
  Pallas kernels  135 us (99%)
    pallas_call x1, Pallas kernels, local(): pl.pallas_call(kernel, out_shape=jax.ShapeDtypeStruct((HEIGHT, ROWS), jnp...  135 us

profile of v10, /device:TPU:1, one launch (start us, length us, event | category | flops | bytes accessed | tf_op | source)
XLA Modules:
  0.0 136.1 jit_solution(7276783512864799371)
XLA Ops:
  0.0 134.7 %shard_map.55 = f32[48,96]{1,0:T(8,128)} custom-call(s32[4,768]{1,0:T(4,128)} %bitcast.1, f32[768]{0:T(1024)} %lmo_energy_in.1, bf16[6,256,768]{2,1,0:T(8,128)(2,1)} %factors.1, bf16[6,256,768]{2,1,0:T(8,128)(2,1)} %integrals.1, f32[768,256]{1,0:T(8,128)} %pao_energy_in.1), custom_call_target="tpu_custom_call" | custom-call | tf_op jit(solution)/shard_map/pallas_call | solution.py:509
  134.8 1.3 copy.7

commit v11 on v9

--- a/solution.py
+++ b/solution.py
@@ -146,11 +146,11 @@
                  (wide_sem.at[0, t - 1], wide_sem.at[1, t - 1]), neighbour(t))
         )
 
-    def send_tiles(chunk):
+    def send_tiles(start):
         for t in range(1, 16):
             end = row_of(t) + HEIGHT
 
-            @pl.when((end > chunk * 256) & (end <= chunk * 256 + 256))
+            @pl.when((end > start) & (end <= start + 128))
             def _():
                 spread[t - 1].start()
 
@@ -161,8 +161,7 @@
         block[pl.ds(0, ROWS), at] = kept + second_in[h, chunk].astype(jnp.float32)
         turned[at, :] = jnp.transpose(block[:, at])
         outgoing[at, :] = turned[at, :].astype(outgoing.dtype)
-        if h == 1:
-            send_tiles(chunk)
+        send_tiles(at.start)
 
     result = turned[rows(0), :]
     for t in range(1, 16):

time: 137 us -> 136 us (level)
  no operation moved by 1% of the time
where the time goes in v11:
time: 136 us
  Pallas kernels  135 us (99%)
    pallas_call x1, Pallas kernels, local(): pl.pallas_call(kernel, out_shape=jax.ShapeDtypeStruct((HEIGHT, ROWS), jnp...  135 us

profile of v11, /device:TPU:1, one launch (start us, length us, event | category | flops | bytes accessed | tf_op | source)
XLA Modules:
  0.0 136.0 jit_solution(10350691764417370723)
XLA Ops:
  0.0 134.7 %shard_map.55 = f32[48,96]{1,0:T(8,128)} custom-call(s32[4,768]{1,0:T(4,128)} %bitcast.1, f32[768]{0:T(1024)} %lmo_energy_in.1, bf16[6,256,768]{2,1,0:T(8,128)(2,1)} %factors.1, bf16[6,256,768]{2,1,0:T(8,128)(2,1)} %integrals.1, f32[768,256]{1,0:T(8,128)} %pao_energy_in.1), custom_call_target="tpu_custom_call" | custom-call | tf_op jit(solution)/shard_map/pallas_call | solution.py:506
  134.7 1.3 copy.7

commit v12 on v11

--- a/solution.py
+++ b/solution.py
@@ -122,7 +122,7 @@
         )
         firsts[h, chunk].start()
     block[pl.ds(ROWS, 128 - ROWS), :] = jnp.zeros((128 - ROWS, AUX), jnp.float32)
-    for h, chunk in chunks:
+    def pass_on(h, chunk):
         near, far, sent = plan[h]
         firsts[h, chunk].wait_recv()
         passed = summed[flip(y, far), :, columns(h, chunk)] + first_in[h, chunk, 1].astype(jnp.float32)
@@ -154,7 +154,7 @@
             def _():
                 spread[t - 1].start()
 
-    for h, chunk in chunks:
+    def finish(h, chunk):
         at = columns(h, chunk)
         kept = summed[y, :, at] + first_in[h, chunk, 0].astype(jnp.float32)
         seconds[h, chunk].wait_recv()
@@ -163,6 +163,11 @@
         outgoing[at, :] = turned[at, :].astype(outgoing.dtype)
         send_tiles(at.start)
 
+    for step in range(len(chunks) + 4):
+        if step < len(chunks):
+            pass_on(*chunks[step])
+        if step >= 4:
+            finish(*chunks[step - 4])
     result = turned[rows(0), :]
     for t in range(1, 16):
         spread[t - 1].wait_recv()

time: 136 us -> 136 us (level)
  no operation moved by 1% of the time
where the time goes in v12:
time: 136 us
  Pallas kernels  135 us (99%)
    pallas_call x1, Pallas kernels, local(): pl.pallas_call(kernel, out_shape=jax.ShapeDtypeStruct((HEIGHT, ROWS), jnp...  135 us

profile of v12, /device:TPU:1, one launch (start us, length us, event | category | flops | bytes accessed | tf_op | source)
XLA Modules:
  0.0 136.0 jit_solution(11649819619342819063)
XLA Ops:
  0.0 134.7 %shard_map.55 = f32[48,96]{1,0:T(8,128)} custom-call(s32[4,768]{1,0:T(4,128)} %bitcast.1, f32[768]{0:T(1024)} %lmo_energy_in.1, bf16[6,256,768]{2,1,0:T(8,128)(2,1)} %factors.1, bf16[6,256,768]{2,1,0:T(8,128)(2,1)} %integrals.1, f32[768,256]{1,0:T(8,128)} %pao_energy_in.1), custom_call_target="tpu_custom_call" | custom-call | tf_op jit(solution)/shard_map/pallas_call | solution.py:511
  134.7 1.3 copy.7
